TPU v7x, 128 devices: a whole 4x4x4 slice. The times are simulated.
128 devices in a mesh: dap: 32 (over z, x_lo, y), rep: 4 (over x_hi, core).
Axes of the slice: x: 4 (x_hi: 2, x_lo: 2; x = x_hi * 2 + x_lo), y: 4, z: 4, core: 2. Of those that a mesh axis runs over, the one named last changes fastest.
Arguments:
- pair_rep: bfloat16 [1024, 1024, 128], P('dap'), may hold values from -6 to 6
- residue_mask: int32 [1024], replicated, may hold values 0 or 1
- pair_mask: int32 [1024, 1024], P('dap'), may hold values 0 or 1
- input_gain: float32 [128], replicated, may hold values from 0.25 to 1.75
- input_bias: float32 [128], replicated, may hold values from -3 to 3
- left_proj: bfloat16 [128, 128], P(None, 'rep'), may hold values from -0.5 to 0.5
- left_gate: bfloat16 [128, 128], P(None, 'rep'), may hold values from -0.5 to 0.5
- right_proj: bfloat16 [128, 128], P(None, 'rep'), may hold values from -0.5 to 0.5
- right_gate: bfloat16 [128, 128], P(None, 'rep'), may hold values from -0.5 to 0.5
- gate_weight: bfloat16 [128, 128], P(None, 'rep'), may hold values from -0.5 to 0.5
- output_gain: float32 [128], replicated, may hold values from 0.25 to 1.75
- output_bias: float32 [128], replicated, may hold values from -3 to 3
- out_weight: bfloat16 [128, 128], replicated, may hold values from -0.5 to 0.5
Outputs:
- update: bfloat16 [128, 1024, 1024], P('rep', None, 'dap')
All inputs are finite; a program needn't handle non-finite values. No bound on the sum of `pair_mask` on one device may be relied on, other than what follows from the above.
Results may differ from a plain program's by a relative error of at most 0.0066.
Values may be sent and summed in bfloat16 or wider, within the bound.
No kernel may reach another device: no remote copies, remote signals or barrier semaphores. Data moves between devices by JAX's collectives and lax.ppermute only.
A program may use at most 192 MiB of HBM per device.

v0:
```python
import jax
import jax.numpy as jnp
from jax import lax
from jax.sharding import PartitionSpec as P

eps = 1e-05


def on_device(
    pair_rep,
    residue_mask,
    pair_mask,
    input_gain,
    input_bias,
    left_proj,
    left_gate,
    right_proj,
    right_gate,
    gate_weight,
    output_gain,
    output_bias,
    out_weight,
):
    rows = pair_rep.shape[0]
    total = pair_rep.shape[1]
    width = pair_rep.shape[2]
    first = lax.axis_index("dap") * rows
    own_residues = lax.dynamic_slice_in_dim(residue_mask, first, rows, 0)
    weights = (own_residues[:, None] * residue_mask[None, :] * pair_mask).astype(jnp.float32)
    values_in = pair_rep.astype(jnp.float32)
    mean_in = jnp.mean(values_in, axis=-1, keepdims=True)
    centred_in = values_in - mean_in
    var_in = jnp.mean(centred_in * centred_in, axis=-1, keepdims=True)
    normed_in = (centred_in * lax.rsqrt(var_in + eps) * input_gain + input_bias).astype(
        jnp.bfloat16
    )
    flat = normed_in.reshape(rows * total, width)

    def project(proj_weight, gate_proj):
        linear = jnp.dot(flat, proj_weight, preferred_element_type=jnp.float32)
        gated = jax.nn.sigmoid(jnp.dot(flat, gate_proj, preferred_element_type=jnp.float32))
        result = (gated * linear).reshape(rows, total, -1) * weights[:, :, None]
        return jnp.transpose(result.astype(jnp.bfloat16), (2, 0, 1))

    left = project(left_proj, left_gate)
    right = project(right_proj, right_gate)
    gating = jax.nn.sigmoid(jnp.dot(flat, gate_weight, preferred_element_type=jnp.float32))
    gating = jnp.transpose(gating.reshape(rows, total, -1).astype(jnp.bfloat16), (2, 0, 1))
    product = jnp.einsum(
        "cik,cjk->cij",
        left,
        lax.all_gather(right, "dap", axis=1, tiled=True),
        preferred_element_type=jnp.float32,
    ).astype(jnp.bfloat16)
    product, gate_cols = (
        lax.all_to_all(product, "dap", split_axis=2, concat_axis=1, tiled=True),
        lax.all_to_all(gating, "dap", split_axis=2, concat_axis=1, tiled=True),
    )
    out_local = gate_cols.shape[0]
    gathered = lax.all_gather(product, "rep", axis=0, tiled=True)
    values = gathered.astype(jnp.float32)
    mean_out = jnp.mean(values, axis=0, keepdims=True)
    centred = values - mean_out
    var_out = jnp.mean(centred * centred, axis=0, keepdims=True)
    normed_out = (
        centred * lax.rsqrt(var_out + eps) * output_gain[:, None, None] + output_bias[:, None, None]
    ).astype(jnp.bfloat16)
    column_part = lax.dynamic_slice_in_dim(
        out_weight, lax.axis_index("rep") * out_local, out_local, 1
    )
    projected = jnp.einsum(
        "hij,hc->cij", normed_out, column_part, preferred_element_type=jnp.float32
    )
    return (gate_cols.astype(jnp.float32) * projected).astype(jnp.bfloat16)


def solution(mesh):
    in_specs = (
        P("dap", None, None),
        P(),
        P("dap", None),
        P(),
        P(),
        P(None, "rep"),
        P(None, "rep"),
        P(None, "rep"),
        P(None, "rep"),
        P(None, "rep"),
        P(),
        P(),
        P(),
    )
    out_specs = P("rep", None, "dap")
    return jax.shard_map(
        on_device, mesh=mesh, in_specs=in_specs, out_specs=out_specs, check_vma=False
    )
```

profile of v0, /device:TPU:1, one launch (start us, length us, event | category | flops | bytes accessed | tf_op | source)
XLA Modules:
  0.0 1048.0 jit_solution(4520359332199409242)
XLA Ops:
  6.6 5.8 convert_reduce_fusion.1
  12.4 11.0 %fusion.18 = f32[32,1024]{1,0:T(8,128)S(1)} fusion(bf16[32,1024,128]{2,1,0:T(8,128)(2,1)} %param.13, f32[32,1024]{1,0:T(8,128)S(1)} %broadcast_multiply_fusion.1), kind=kLoop, calls=%fused_computation.27 | loop fusion | flops 16744448 | bytes 8650752 | tf_op jit(solution)/shard_map/reduce_sum | solution.py:33
  23.5 10.3 fusion.21
  39.8 4.4 copy.27
  50.2 4.8 copy.26
  55.2 6.1 fusion.25
  61.3 716.5 %all-gather.3.cloned.1.call-done = bf16[32,1024,1024]{2,1,0:T(8,128)(2,1)} async-done(((bf16[32,32,1024]{2,1,0:T(8,128)(2,1)}), bf16[32,1024,1024]{2,1,0:T(8,128)(2,1)}) %all-gather.3.cloned.1.call-update) | async-done | bytes 67108880 | tf_op jit(solution)/shard_map/all_gather | solution.py:52
  777.8 28.2 %fusion.30 = bf16[32,32,1024]{2,1,0:T(8,128)(2,1)} fusion(bf16[32,1024,1024]{2,1,0:T(8,128)(2,1)} %all-gather.3.cloned.1.call-done, bf16[32,1024,32]{1,0,2:T(8,128)(2,1)S(1)} %get-tuple-element.5), kind=kOutput, calls=%fused_computation.40 | convolution fusion | flops 2148532224 | bytes 71303168 | tf_op jit(solution)/shard_map/cik,cjk->cij/dot_general | solution.py:49
  806.0 12.5 %copy.21 = bf16[32,32,1024]{1,0,2:T(8,128)(2,1)} copy(bf16[32,32,1024]{2,1,0:T(8,128)(2,1)} %fusion.30) | data formatting | bytes 4194304 | tf_op jit(solution)/shard_map/convert_element_type | solution.py:54
  818.5 12.2 %reshape.54 = bf16[32,2,16384]{2,1,0:T(2,128)(2,1)S(1)} reshape(bf16[1024,32,32]{2,1,0:T(8,128)(2,1)} %bitcast.72) | data formatting | bytes 4194304
  830.8 30.5 %all_to_all.27 = bf16[32,2,16384]{2,1,0:T(2,128)(2,1)} all-to-all(bf16[32,2,16384]{2,1,0:T(2,128)(2,1)S(1)} %reshape.54), channel_id=1, replica_groups=mesh['dap'=32,'rep'=4] {'dap'}, dimensions={0} | all-to-all | bytes 4194304 | tf_op jit(solution)/shard_map/all_to_all | solution.py:56
  861.3 11.8 %reshape.55 = bf16[1024,32,32]{2,1,0:T(8,128)(2,1)} reshape(bf16[32,2,16384]{2,1,0:T(2,128)(2,1)} %all_to_all.27) | data formatting | bytes 4194304
  873.1 16.3 %copy.22 = bf16[32,32,32,32]{2,1,0,3:T(8,128)(2,1)} copy(bf16[32,32,32,32]{2,0,3,1:T(8,128)(2,1)} %bitcast.73) | data formatting | bytes 4194304 | tf_op jit(solution)/shard_map/all_to_all | solution.py:56
  889.4 12.5 %all_to_all.24 = bf16[32,1024,32]{1,0,2:T(8,128)(2,1)} reshape(bf16[32,32,32,32]{2,1,0,3:T(8,128)(2,1)} %copy.22) | data formatting | bytes 4194304 | tf_op jit(solution)/shard_map/all_to_all | solution.py:56
  902.0 6.4 fusion.7
  909.5 12.1 %copy.18 = bf16[32,1024,32]{0,2,1:T(8,128)(2,1)} copy(bf16[32,1024,32]{1,0,2:T(8,128)(2,1)S(1)} %bitcast.77) | data formatting | bytes 4194304 | tf_op jit(solution)/shard_map/convert_element_type | solution.py:48
  921.7 8.1 bitcast_bitcast_fusion
  929.8 13.3 %reshape.52 = bf16[32,2,16384]{2,1,0:T(2,128)(2,1)} reshape(bf16[1024,32,32]{2,1,0:T(8,128)(2,1)} %bitcast_bitcast_fusion) | data formatting | bytes 4194304
  943.1 6.4 all-to-all-start
  949.5 36.6 %all-to-all-done = bf16[32,2,16384]{2,1,0:T(2,128)(2,1)S(1)} async-done(((bf16[32,2,16384]{2,1,0:T(2,128)(2,1)}), bf16[32,2,16384]{2,1,0:T(2,128)(2,1)S(1)}, u32[]{:S(2)}, u32[]{:S(2)}) %all-to-all-start) | async-done | bytes 2097184 | tf_op jit(solution)/shard_map/all_to_all | solution.py:57
  986.1 6.6 reshape.53
  992.6 18.8 %copy.29 = f32[32,32,32,32]{1,2,0,3:T(8,128)} copy(bf16[32,32,32,32]{1,0,3,2:T(8,128)(2,1)} %bitcast.71) | data formatting | bytes 6291456 | tf_op jit(solution)/shard_map/convert_element_type | solution.py:74
  1011.5 13.9 %reshape.49 = f32[32,1024,32]{1,0,2:T(8,128)} reshape(f32[32,32,32,32]{2,1,0,3:T(8,128)} %bitcast.70) | data formatting | bytes 8388608 | tf_op jit(solution)/shard_map/convert_element_type | solution.py:74
  1025.4 5.8 convert_reduce_fusion
  (54 shorter events, 23.0 us)
Async XLA Ops:
  6.5 1027.5 %copy-start = (bf16[128,128]{1,0:T(8,128)(2,1)S(1)}, bf16[128,128]{1,0:T(8,128)(2,1)}, u32[]{:S(2)}) copy-start(bf16[128,128]{1,0:T(8,128)(2,1)} %param.25) | copy-start | bytes 98308
  6.5 771.3 %all-gather.3.cloned.1.call-start = ((), (), s32[]{:S(2)}) async-start(), calls=%async_computation.2 | async-start | bytes 69206016 | tf_op jit(solution)/shard_map/all_gather | solution.py:52
  6.5 16.9 %slice-start = ((s8[8388608]{0:T(1024)(128)(4,1)}), s8[4194304]{0:T(1024)(128)(4,1)S(1)}, s32[]{:S(2)}) async-start(s8[8388608]{0:T(1024)(128)(4,1)} %bitcast.68), calls=%async_computation.4 | async-start | bytes 8388608
  6.5 16.9 %copy-start.8 = (f32[128]{0:T(128)S(1)}, f32[128]{0:T(128)}, u32[]{:S(2)}) copy-start(f32[128]{0:T(128)} %param.17) | copy-start | bytes 1540
  6.5 16.9 %copy-start.9 = (f32[128]{0:T(128)S(1)}, f32[128]{0:T(128)}, u32[]{:S(2)}) copy-start(f32[128]{0:T(128)} %param.16) | copy-start | bytes 1540
  12.4 11.0 %slice-start.1 = ((s8[8388608]{0:T(1024)(128)(4,1)}), s8[4194304]{0:T(1024)(128)(4,1)S(1)}, s32[]{:S(2)}) async-start(s8[8388608]{0:T(1024)(128)(4,1)} %bitcast.68), calls=%async_computation.5 | async-start | bytes 8388608
  23.4 10.3 copy-start.10
  33.7 13.4 %copy-start.1 = (bf16[32,1024,128]{2,1,0:T(8,128)(2,1)}, bf16[32,1024,128]{2,1,0:T(8,128)(2,1)S(1)}, u32[]{:S(2)}) copy-start(bf16[32,1024,128]{2,1,0:T(8,128)(2,1)S(1)} %fusion.21) | copy-start | bytes 25165828
  33.8 3.0 copy-start.5
  39.8 4.4 copy-start.11
  44.2 3.0 copy-start.6
  50.2 4.8 copy-start.7
  50.2 4.9 copy-start.4
  61.3 964.1 %all-gather.5.cloned.1.call-start = ((), (), s32[]{:S(2)}) async-start(), calls=%async_computation.3 | async-start | bytes 10485760 | tf_op jit(solution)/shard_map/all_gather | solution.py:60
  889.4 12.6 %copy-start.12 = (bf16[128,32]{0,1:T(8,128)(2,1)S(1)}, bf16[128,32]{0,1:T(8,128)(2,1)}, u32[]{:S(2)}) copy-start(bf16[128,32]{0,1:T(8,128)(2,1)} %param.22) | copy-start | bytes 24580
  943.1 42.9 %all-to-all-start = ((bf16[32,2,16384]{2,1,0:T(2,128)(2,1)}), bf16[32,2,16384]{2,1,0:T(2,128)(2,1)S(1)}, u32[]{:S(2)}, u32[]{:S(2)}) async-start(bf16[32,2,16384]{2,1,0:T(2,128)(2,1)} %reshape.52), calls=%async_computation | async-start | bytes 4194304 | tf_op jit(solution)/shard_map/all_to_all | solution.py:57
  1025.4 8.7 copy-start.13
  1025.4 8.7 copy-start.14
  1025.4 5.8 copy-start.2
  1025.4 8.7 copy-start.3
Sparse Core Ops, SparseCore 0:
  61.4 716.3 all-gather.2
  902.1 71.2 all-gather.4
where the time goes:
time: 1050 us
  waiting for transfers between devices  753 us (72%)
  local copies, waits for them, and re-layouts  151 us (14%)
  matrix products  50.8 us (5%)
  other arithmetic  41.8 us (4%)
  blocking collectives  30.5 us (3%)
  between operations  14 us (1%)
    all_gather x1, waiting for transfers between devices, on_device(): lax.all_gather(right, 'dap', axis=1, tiled=True)  717 us
    unnamed x42, local copies, waits for them, and re-layouts  62.5 us
    all_to_all x1, waiting for transfers between devices, on_device(): lax.all_to_all(gating, 'dap', split_axis=2, concat_axis=1, tiled=True)  36.6 us
    convert_element_type x3, local copies, waits for them, and re-layouts, on_device(): return (gate_cols.astype(jnp.float32) * projected).astype(jnp.bfloat16)  35.2 us
    all_to_all x1, blocking collectives, on_device(): lax.all_to_all(product, 'dap', split_axis=2, concat_axis=1, tiled=True)  30.5 us
    all_to_all x2, local copies, waits for them, and re-layouts, on_device(): lax.all_to_all(product, 'dap', split_axis=2, concat_axis=1, tiled=True)  28.9 us
    dot_general x1, matrix products, on_device(): jnp.einsum('cik,cjk->cij', left, lax.all_gather(right, 'dap', axis=1, til...  28.2 us
  transfers between devices with their start and end apart: 3, of which 2 were waited for; matrix products, arithmetic and copies ran while one was open for 8% of the time, Pallas kernels for 0%

commit v1 on v0

v1 whole, which is shorter than its diff:
```python
import jax
import jax.numpy as jnp
from jax import lax
from jax.experimental import pallas as pl
from jax.experimental.pallas import tpu as pltpu
from jax.sharding import PartitionSpec as P

eps = 1e-05
bf16 = jnp.bfloat16
f32 = jnp.float32
everyone = ("dap", "rep")
lane = 128


def params(mib=48):
    return pltpu.CompilerParams(vmem_limit_bytes=mib * 2**20)


def sigmoid(x):
    return 0.5 * jnp.tanh(0.5 * x) + 0.5


def rows_by_rows(a, b):
    return lax.dot_general(a, b, (((1,), (1,)), ((), ())), preferred_element_type=f32)


def norm_kernel(where, x_ref, gain_ref, bias_ref, out_ref):
    x = x_ref[...].astype(f32)
    width = x.shape[-1]
    mean = jnp.sum(x, axis=-1, keepdims=True) * (1.0 / width)
    centred = x - mean
    var = jnp.sum(centred * centred, axis=-1, keepdims=True) * (1.0 / width)
    out_ref[...] = (centred * lax.rsqrt(var + eps) * gain_ref[...] + bias_ref[...]).astype(bf16)


def norm_in(where, pair_rep, gain, bias, share, tile):
    rows, total, width = pair_rep.shape
    return pl.pallas_call(
        norm_kernel,
        grid_spec=pltpu.PrefetchScalarGridSpec(
            num_scalar_prefetch=1,
            grid=(total // tile,),
            in_specs=[
                pl.BlockSpec((share, tile, width), lambda t, where: (where[1], t, 0)),
                pl.BlockSpec((1, 1, width), lambda t, where: (0, 0, 0)),
                pl.BlockSpec((1, 1, width), lambda t, where: (0, 0, 0)),
            ],
            out_specs=pl.BlockSpec((share, tile, width), lambda t, where: (0, t, 0)),
        ),
        out_shape=jax.ShapeDtypeStruct((share, total, width), bf16),
        compiler_params=params(),
        name="norm_in",
    )(where, pair_rep, gain.reshape(1, 1, width), bias.reshape(1, 1, width))


def project_kernel(where, residues, x_ref, w_ref, keep_ref, mask_ref, out_ref, held):
    share, tile, width = x_ref.shape
    hidden = out_ref.shape[0]
    lanes = mask_ref[...].astype(f32)
    keep = keep_ref[...].astype(f32) * lanes
    first = where[0] * share
    for i in range(share):
        x = x_ref[i]
        weight = keep[i : i + 1, :] * residues[first + i].astype(f32)
        for side in range(2):
            linear = rows_by_rows(w_ref[:, 2 * side].reshape(hidden, width), x)
            gate = rows_by_rows(w_ref[:, 2 * side + 1].reshape(hidden, width), x)
            result = sigmoid(gate) * linear * weight
            for part in range(tile // lane):
                held[side, part, pl.ds(i, hidden, stride=share), :] = result[
                    :, part * lane : (part + 1) * lane
                ]
    for side in range(2):
        for part in range(tile // lane):
            out_ref[
                :, side * share : (side + 1) * share, part * lane : (part + 1) * lane
            ] = held[side, part].reshape(hidden, share, lane).astype(bf16)


def project(where, residue_mask, normed, weights, pair_mask, tile):
    share, total, width = normed.shape
    hidden = weights.shape[0] * weights.shape[2]
    return pl.pallas_call(
        project_kernel,
        grid_spec=pltpu.PrefetchScalarGridSpec(
            num_scalar_prefetch=2,
            grid=(total // tile,),
            in_specs=[
                pl.BlockSpec((share, tile, width), lambda t, *_: (0, t, 0)),
                pl.BlockSpec(weights.shape, lambda t, *_: (0, 0, 0, 0)),
                pl.BlockSpec((share, tile), lambda t, where, _: (where[1], t)),
                pl.BlockSpec((1, tile), lambda t, *_: (0, t)),
            ],
            out_specs=pl.BlockSpec((hidden, 2 * share, tile), lambda t, *_: (0, 0, t)),
            scratch_shapes=[pltpu.VMEM((2, tile // lane, hidden * share, lane), f32)],
        ),
        out_shape=jax.ShapeDtypeStruct((hidden, 2 * share, total), bf16),
        compiler_params=params(),
        name="project",
    )(where, residue_mask, normed, weights, pair_mask, residue_mask.reshape(1, total))


def gate_kernel(x_ref, w_ref, out_ref):
    width = x_ref.shape[-1]
    w = w_ref[:, 4].reshape(-1, width)
    for i in range(x_ref.shape[0]):
        out_ref[i] = sigmoid(rows_by_rows(w, x_ref[i])).astype(bf16)


def gates(normed, weights, tile):
    share, total, width = normed.shape
    channels = weights.shape[0] * weights.shape[2]
    return pl.pallas_call(
        gate_kernel,
        grid=(total // tile,),
        in_specs=[
            pl.BlockSpec((share, tile, width), lambda t: (0, t, 0)),
            pl.BlockSpec(weights.shape, lambda t: (0, 0, 0, 0)),
        ],
        out_specs=pl.BlockSpec((share, channels, tile), lambda t: (0, 0, t)),
        out_shape=jax.ShapeDtypeStruct((share, channels, total), bf16),
        compiler_params=params(),
        cost_estimate=pl.CostEstimate(
            flops=2 * share * total * width * channels,
            bytes_accessed=4 * share * total * width,
            transcendentals=share * total * channels,
        ),
        name="gates",
    )(normed, weights)


def product_kernel(left_ref, right_ref, out_ref):
    blocks, two, total = left_ref.shape
    share = two // 2
    left = left_ref[:, :share, :].reshape(blocks * share, total)
    right = right_ref[:, share:, :].reshape(-1, total)
    out_ref[...] = rows_by_rows(left, right).astype(bf16).reshape(out_ref.shape)


def products(both, tile):
    blocks, two, total = both.shape
    return pl.pallas_call(
        product_kernel,
        grid=(blocks // tile,),
        in_specs=[
            pl.BlockSpec((tile, two, total), lambda t: (t, 0, 0)),
            pl.BlockSpec(both.shape, lambda t: (0, 0, 0)),
        ],
        out_specs=pl.BlockSpec((tile, two // 2, total), lambda t: (t, 0, 0)),
        out_shape=jax.ShapeDtypeStruct((blocks, two // 2, total), bf16),
        compiler_params=params(),
        name="products",
    )(both, both)


def update_kernel(p_ref, gate_ref, gain_ref, bias_ref, w_ref, out_ref, held, placed):
    hidden, share, tile = p_ref.shape
    channels = w_ref.shape[0]
    pack, span = 4, tile // 4
    values = p_ref[...].astype(f32)
    mean = jnp.sum(values, axis=0, keepdims=True) * (1.0 / hidden)
    centred = values - mean
    var = jnp.sum(centred * centred, axis=0, keepdims=True) * (1.0 / hidden)
    normed = centred * lax.rsqrt(var + eps) * gain_ref[...] + bias_ref[...]
    held[...] = normed.reshape(hidden * share, tile)
    for i in range(share):
        row = held[pl.ds(i, hidden, stride=share), :].astype(bf16)
        projected = jnp.dot(w_ref[...], row, preferred_element_type=f32)
        placed[pl.ds(i, channels, stride=share), :] = gate_ref[i].astype(f32) * projected
    result = placed[...].reshape(channels // pack, pack, share, tile)
    for block in range(pack):
        piece = jnp.concatenate(
            [result[:, c, :, block * span : (block + 1) * span] for c in range(pack)], axis=-1
        )
        out_ref[block] = piece.astype(bf16).reshape(out_ref.shape[1:])


def updates(product, gating, gain, bias, out_weight_t):
    hidden, share, total = product.shape
    channels = out_weight_t.shape[0]
    tile = 128
    rows = channels * share // 4
    return pl.pallas_call(
        update_kernel,
        grid=(total // tile,),
        in_specs=[
            pl.BlockSpec((hidden, share, tile), lambda t: (0, 0, t)),
            pl.BlockSpec((share, channels, tile), lambda t: (0, 0, t)),
            pl.BlockSpec((hidden, 1, 1), lambda t: (0, 0, 0)),
            pl.BlockSpec((hidden, 1, 1), lambda t: (0, 0, 0)),
            pl.BlockSpec((channels, hidden), lambda t: (0, 0)),
        ],
        out_specs=pl.BlockSpec((4, rows, tile), lambda t: (t, 0, 0)),
        out_shape=jax.ShapeDtypeStruct((total // 32, rows, tile), bf16),
        scratch_shapes=[
            pltpu.VMEM((hidden * share, tile), f32),
            pltpu.VMEM((channels * share, tile), f32),
        ],
        compiler_params=params(),
        name="updates",
    )(product, gating, gain.reshape(hidden, 1, 1), bias.reshape(hidden, 1, 1), out_weight_t)


def place_kernel(u_ref, out_ref):
    blocks, share, lanes = u_ref.shape
    flat = u_ref[...].astype(f32).reshape(blocks * share, lanes)
    out_ref[...] = flat.T.astype(bf16).reshape(out_ref.shape)


def place(received, share):
    blocks, rows, lanes = received.shape
    groups = rows // share
    return pl.pallas_call(
        place_kernel,
        grid=(groups,),
        in_specs=[pl.BlockSpec((blocks, share, lanes), lambda g: (0, g, 0))],
        out_specs=pl.BlockSpec((4, lanes // 4, blocks * share), lambda g: (g, 0, 0)),
        out_shape=jax.ShapeDtypeStruct((groups * 4, lanes // 4, blocks * share), bf16),
        compiler_params=params(),
        name="place",
    )(received)


def exchange(blocks):
    return lax.all_to_all(blocks, everyone, split_axis=0, concat_axis=0, tiled=True)


def on_device(
    pair_rep,
    residue_mask,
    pair_mask,
    input_gain,
    input_bias,
    left_proj,
    left_gate,
    right_proj,
    right_gate,
    gate_weight,
    output_gain,
    output_bias,
    out_weight,
):
    rows = pair_rep.shape[0]
    parts = lax.axis_size("rep")
    share = rows // parts
    own = lax.axis_index("rep")
    where = jnp.stack([lax.axis_index("dap") * parts + own, own]).astype(jnp.int32)
    weights = jnp.stack([left_proj.T, left_gate.T, right_proj.T, right_gate.T, gate_weight.T])
    weights = lax.all_gather(weights, "rep", axis=0)
    normed = norm_in(where, pair_rep, input_gain, input_bias, share, 256)
    both = project(where, residue_mask, normed, weights, pair_mask, 256)
    both = exchange(both)
    gating = gates(normed, weights, 256)
    product = exchange(products(both, 32))
    update = updates(product, gating, output_gain, output_bias, out_weight.T)
    total, tile = product.shape[0], update.shape[-1]
    update = exchange(update.reshape(total, -1, tile))
    return jnp.swapaxes(place(update, share), 1, 2)


def solution(mesh):
    in_specs = (
        P("dap", None, None),
        P(),
        P("dap", None),
        P(),
        P(),
        P(None, "rep"),
        P(None, "rep"),
        P(None, "rep"),
        P(None, "rep"),
        P(None, "rep"),
        P(),
        P(),
        P(),
    )
    out_specs = P("rep", None, "dap")
    return jax.shard_map(
        on_device, mesh=mesh, in_specs=in_specs, out_specs=out_specs, check_vma=False
    )
```

time: 1050 us -> 179 us (0.17)
  waiting for transfers between devices: 753 us -> 26.2 us
  local copies, waits for them, and re-layouts: 151 us -> 7.8 us
  blocking collectives: 30.5 us -> 106 us
  matrix products: 50.8 us -> 0 us
  other arithmetic: 41.8 us -> 0.07 us
  Pallas kernels: 0 us -> 31.3 us
  between operations: 14 us -> 0.11 us
    all_gather x2 -> x0, waiting for transfers between devices: 717 us -> none  [the longest x1 717 us: on_device(): lax.all_gather(right, 'dap', axis=1, tiled=True)]
    all_to_all x1 -> x2, blocking collectives: 30.5 us -> 97.3 us  [exchange(): lax.all_to_all(blocks, everyone, split_axis=0, concat_axis=0, tiled=True)]
    convert_element_type x5 -> x0, local copies, waits for them, and re-layouts: 59.9 us -> none  [the longest x3 35.2 us: on_device(): return (gate_cols.astype(jnp.float32) * projected).astype(jnp.bfloat16)]
    unnamed x42 -> x23, local copies, waits for them, and re-layouts: 62.5 us -> 6.88 us
    dot_general x7 -> x0, matrix products: 50.8 us -> none  [the longest x1 28.2 us: on_device(): jnp.einsum('cik,cjk->cij', left, lax.all_gather(right, 'dap', axis=1, til...]
    pallas_call x0 -> x6, Pallas kernels: none -> 31.3 us  [the longest x1 8.86 us: updates(): pl.pallas_call(update_kernel, grid=(total // tile,), in_specs=[pl.BlockSp...]
    all_to_all x2 -> x0, local copies, waits for them, and re-layouts: 28.9 us -> none  [on_device(): lax.all_to_all(product, 'dap', split_axis=2, concat_axis=1, tiled=True)]
    reduce_sum x4 -> x0, other arithmetic: 25.3 us -> none  [the longest x1 11 us: on_device(): var_in = jnp.mean(centred_in * centred_in, axis=-1, keepdims=True)]
  transfers between devices with their start and end apart: 3 -> 1, of which waited for: 2 -> 1; matrix products, arithmetic and copies ran while one was open for 8% -> 0% of each run, Pallas kernels for 0% -> 1%
where the time goes in v1:
time: 179 us; the launch traced here: 178 us
  blocking collectives  106 us (59%)
  Pallas kernels  31.3 us (17%)
  waiting for transfers between devices  26.2 us (15%)
  local copies, waits for them, and re-layouts  7.8 us (4%)
  starting transfers between devices  7.38 us (4%)
    all_to_all x2, blocking collectives, exchange(): lax.all_to_all(blocks, everyone, split_axis=0, concat_axis=0, tiled=True)  97.3 us
    all_to_all x1, waiting for transfers between devices, exchange(): lax.all_to_all(blocks, everyone, split_axis=0, concat_axis=0, tiled=True)  26.2 us
    pallas_call x1, Pallas kernels, updates(): pl.pallas_call(update_kernel, grid=(total // tile,), in_specs=[pl.BlockSp...  8.86 us
    all_gather x1, blocking collectives, on_device(): weights = lax.all_gather(weights, 'rep', axis=0)  8.26 us
    all_to_all x1, starting transfers between devices, exchange(): lax.all_to_all(blocks, everyone, split_axis=0, concat_axis=0, tiled=True)  7.38 us
    unnamed x23, local copies, waits for them, and re-layouts  6.88 us
    pallas_call x1, Pallas kernels, products(): pl.pallas_call(product_kernel, grid=(blocks // tile,), in_specs=[pl.Block...  6.24 us
    pallas_call x1, Pallas kernels, project(): pl.pallas_call(project_kernel, grid_spec=pltpu.PrefetchScalarGridSpec(num...  5.83 us
  transfers between devices with their start and end apart: 1, of which 1 were waited for; matrix products, arithmetic and copies ran while one was open for 0% of the time, Pallas kernels for 1%

profile of v1, /device:TPU:1, one launch (start us, length us, event | category | flops | bytes accessed | tf_op | source)
XLA Modules:
  0.0 178.5 jit_solution(18227476216506818219)
XLA Ops:
  0.0 0.7 constant_dynamic-update-slice_fusion.4
  0.7 0.7 constant_dynamic-update-slice_fusion.3
  1.4 0.7 constant_dynamic-update-slice_fusion.2
  2.1 0.7 constant_dynamic-update-slice_fusion.1
  2.8 0.7 constant_dynamic-update-slice_fusion
  3.5 8.3 %all-gather = bf16[20,32,128]{2,1,0:T(8,128)(2,1)S(1)} all-gather(bf16[5,32,128]{2,1,0:T(8,128)(2,1)S(1)} %constant_dynamic-update-slice_fusion), channel_id=2, replica_groups=mesh['dap'=32,'rep'=4] {'rep'}, dimensions={0}, use_global_device_ids=true | all-gather | bytes 204800 | tf_op jit(solution)/shard_map/all_gather | solution.py:249
  11.8 0.1 pad_add_fusion.where
  11.9 0.7 copy-done.4
  12.5 0.7 copy-done.5
  13.2 4.8 %norm_in.1.x_ref = bf16[8,1024,128]{2,1,0:T(8,128)(2,1)S(1)} custom-call(s32[2]{0:T(128)S(1)} %pad_add_fusion.where, bf16[32,1024,128]{2,1,0:T(8,128)(2,1)} %x_ref.1, f32[1,1,128]{2,1,0:T(1,128)S(1)} %bitcast.36, f32[1,1,128]{2,1,0:T(1,128)S(1)} %bitcast.37), custom_call_target="tpu_custom_call" | custom-call | tf_op jit(solution)/shard_map/norm_in/pallas_call | solution.py:38
  18.0 5.8 %project.1 = bf16[128,16,1024]{2,1,0:T(8,128)(2,1)} custom-call(s32[2]{0:T(128)S(1)} %pad_add_fusion.where, s32[1024]{0:T(1024)S(1)} %copy-done.3, bf16[8,1024,128]{2,1,0:T(8,128)(2,1)S(1)} %norm_in.1.x_ref, bf16[4,5,32,128]{3,2,1,0:T(8,128)(2,1)S(1)} %bitcast.32, s32[32,1024]{1,0:T(8,128)S(1)} %copy-done.2, s32[1,1024]{1,0:T(1,128)S(1)} %bitcast.35), custom_call_target="tpu_custom_call" | custom-call | tf_op jit(solution)/shard_map/project/pallas_call | solution.py:83
  23.8 62.7 %all_to_all.15.left_ref.right_ref = bf16[128,16,1024]{2,1,0:T(8,128)(2,1)} all-to-all(bf16[128,16,1024]{2,1,0:T(8,128)(2,1)} %project.1), channel_id=1, replica_groups=mesh['dap'=32,'rep'=4] {'dap','rep'}, dimensions={0} | all-to-all | bytes 8388608 | tf_op jit(solution)/shard_map/all_to_all | solution.py:225
  86.5 6.2 %products.1 = bf16[128,8,1024]{2,1,0:T(8,128)(2,1)S(1)} custom-call(bf16[128,16,1024]{2,1,0:T(8,128)(2,1)} %all_to_all.15.left_ref.right_ref, bf16[128,16,1024]{2,1,0:T(8,128)(2,1)} %all_to_all.15.left_ref.right_ref), custom_call_target="tpu_custom_call" | custom-call | tf_op jit(solution)/shard_map/products/pallas_call | solution.py:142
  92.7 1.3 copy-done
  94.0 7.4 %all-to-all-start.1 = ((bf16[128,8,1024]{2,1,0:T(8,128)(2,1)}), bf16[128,8,1024]{2,1,0:T(8,128)(2,1)}, u32[]{:S(2)}, u32[]{:S(2)}) async-start(bf16[128,8,1024]{2,1,0:T(8,128)(2,1)} %copy-done), calls=%async_computation.1 | async-start | bytes 4194304 | tf_op jit(solution)/shard_map/all_to_all | solution.py:225
  101.4 0.1 copy.17
  101.6 0.1 copy.18.gain_ref
  101.7 0.1 copy.19.bias_ref
  101.8 1.7 gates.1.gate_ref
  103.5 1.3 copy-done.1
  104.8 26.2 %all-to-all-done.1.p_ref = bf16[128,8,1024]{2,1,0:T(8,128)(2,1)} async-done(((bf16[128,8,1024]{2,1,0:T(8,128)(2,1)}), bf16[128,8,1024]{2,1,0:T(8,128)(2,1)}, u32[]{:S(2)}, u32[]{:S(2)}) %all-to-all-start.1) | async-done | bytes 2097184 | tf_op jit(solution)/shard_map/all_to_all | solution.py:225
  131.1 8.9 %updates.1 = bf16[32,256,128]{2,1,0:T(8,128)(2,1)S(1)} custom-call(bf16[128,8,1024]{2,1,0:T(8,128)(2,1)} %all-to-all-done.1.p_ref, bf16[8,128,1024]{2,1,0:T(8,128)(2,1)} %copy-done.1, f32[128,1,1]{2,1,0:T(1,128)S(1)} %copy.18.gain_ref, f32[128,1,1]{2,1,0:T(1,128)S(1)} %copy.19.bias_ref, bf16[128,128]{1,0:T(8,128)(2,1)S(1)} %bitcast.34), custom_call_target="tpu_custom_call" | custom-call | tf_op jit(solution)/shard_map/updates/pallas_call | solution.py:183
  140.0 34.6 %all_to_all.16.u_ref = bf16[128,64,128]{2,1,0:T(8,128)(2,1)S(1)} all-to-all(bf16[128,64,128]{2,1,0:T(8,128)(2,1)S(1)} %bitcast.31), channel_id=1, replica_groups=mesh['dap'=32,'rep'=4] {'dap','rep'}, dimensions={0} | all-to-all | bytes 4194304 | tf_op jit(solution)/shard_map/all_to_all | solution.py:225
  174.6 3.9 %place.1 = bf16[32,32,1024]{2,1,0:T(8,128)(2,1)} custom-call(bf16[128,64,128]{2,1,0:T(8,128)(2,1)S(1)} %all_to_all.16.u_ref), custom_call_target="tpu_custom_call" | custom-call | tf_op jit(solution)/shard_map/place/pallas_call | solution.py:213
  (14 shorter events, 0.0 us)
Async XLA Ops:
  11.8 0.7 copy-start.4
  12.5 0.7 copy-start.5
  13.2 4.8 %copy-start.2 = (s32[32,1024]{1,0:T(8,128)S(1)}, s32[32,1024]{1,0:T(8,128)}, u32[]{:S(2)}) copy-start(s32[32,1024]{1,0:T(8,128)} %keep_ref.1) | copy-start | bytes 393220
  13.2 4.8 %copy-start.3 = (s32[1024]{0:T(1024)S(1)}, s32[1024]{0:T(1024)}, u32[]{:S(2)}) copy-start(s32[1024]{0:T(1024)} %residues.1) | copy-start | bytes 12292
  92.7 1.3 copy-start
  94.0 7.4 %copy-start.6 = (bf16[128,128]{1,0:T(8,128)(2,1)S(1)}, bf16[128,128]{1,0:T(8,128)(2,1)}, u32[]{:S(2)}) copy-start(bf16[128,128]{1,0:T(8,128)(2,1)} %param.25) | copy-start | bytes 98308
  94.0 7.5 %copy-start.7 = (f32[128]{0:T(128)S(1)}, f32[128]{0:T(128)}, u32[]{:S(2)}) copy-start(f32[128]{0:T(128)} %param.23) | copy-start | bytes 1540
  94.0 7.6 %copy-start.8 = (f32[128]{0:T(128)S(1)}, f32[128]{0:T(128)}, u32[]{:S(2)}) copy-start(f32[128]{0:T(128)} %param.24) | copy-start | bytes 1540
  94.0 37.1 %all-to-all-start.1 = ((bf16[128,8,1024]{2,1,0:T(8,128)(2,1)}), bf16[128,8,1024]{2,1,0:T(8,128)(2,1)}, u32[]{:S(2)}, u32[]{:S(2)}) async-start(bf16[128,8,1024]{2,1,0:T(8,128)(2,1)} %copy-done), calls=%async_computation.1 | async-start | bytes 4194304 | tf_op jit(solution)/shard_map/all_to_all | solution.py:225
  103.5 1.3 copy-start.1

commit v2 on v0

v2 whole, which is shorter than its diff:
```python
import jax
import jax.numpy as jnp
from jax import lax
from jax.experimental import pallas as pl
from jax.experimental.pallas import tpu as pltpu
from jax.sharding import PartitionSpec as P

eps = 1e-05
bf16 = jnp.bfloat16
f32 = jnp.float32
everyone = ("dap", "rep")
lane = 128
pack = 4


def params(mib):
    return pltpu.CompilerParams(vmem_limit_bytes=mib * 2**20)


def stay(array):
    return pltpu.with_memory_space_constraint(array, pltpu.HBM)


def rows_by_rows(a, b):
    return lax.dot_general(a, b, (((1,), (1,)), ((), ())), preferred_element_type=f32)


def column(row):
    return jnp.broadcast_to(row, (lane, lane)).T


def widen(column, tile):
    return column if tile == lane else jnp.concatenate([column] * (tile // lane), -1)


def centring(width):
    row = lax.broadcasted_iota(jnp.int32, (width, width), 0)
    at = lax.broadcasted_iota(jnp.int32, (width, width), 1)
    return ((row == at).astype(f32) - 1.0 / width).astype(bf16)


def normed_columns(x, gain, bias):
    width = x.shape[1]
    centred = rows_by_rows(centring(width), x)
    var = jnp.sum(centred * centred, axis=0, keepdims=True) * (1.0 / width)
    return (centred * lax.rsqrt(var + eps) * gain + bias).astype(bf16)


def project_kernel(
    where,
    residues,
    x_ref,
    left_proj,
    left_gate,
    right_proj,
    right_gate,
    gain_ref,
    bias_ref,
    keep_ref,
    mask_ref,
    out_ref,
    held,
):
    rows, tile, width = x_ref.shape
    hidden = out_ref.shape[0]
    step = rows + 1
    weights = jnp.concatenate(
        [left_proj[...], left_gate[...], right_proj[...], right_gate[...]], 0
    )
    lanes = mask_ref[...].astype(f32)
    gain = widen(column(gain_ref[...]), tile)
    bias = widen(column(bias_ref[...]), tile)
    first = where[0] * rows
    for i in range(rows):
        y = jnp.dot(weights, normed_columns(x_ref[i], gain, bias), preferred_element_type=f32)
        keep = keep_ref[i : i + 1, :].astype(f32) * lanes * residues[first + i].astype(f32)
        half = keep * 0.5
        for side in range(2):
            linear = y[2 * side * hidden : (2 * side + 1) * hidden]
            gate = y[(2 * side + 1) * hidden : (2 * side + 2) * hidden]
            result = (jnp.tanh(gate * 0.5) + 1.0) * (linear * half)
            for part in range(tile // lane):
                held[side, part, pl.ds(i, hidden, stride=step), :] = result[
                    :, part * lane : (part + 1) * lane
                ]
    for side in range(2):
        for part in range(tile // lane):
            for c in range(hidden):
                out_ref[c, side, :, part * lane : (part + 1) * lane] = held[
                    side, part, pl.ds(c * step, rows), :
                ].astype(bf16)


def project(where, residue_mask, pair_rep, weights, gain, bias, pair_mask, tile):
    rows, total, width = pair_rep.shape
    hidden = weights[0].shape[0]

    def fixed(t, *_):
        return (0, 0)

    return pl.pallas_call(
        project_kernel,
        grid_spec=pltpu.PrefetchScalarGridSpec(
            num_scalar_prefetch=2,
            grid=(total // tile,),
            in_specs=[
                pl.BlockSpec((rows, tile, width), lambda t, *_: (0, t, 0)),
                *[pl.BlockSpec((hidden, width), fixed)] * 4,
                *[pl.BlockSpec((1, width), fixed)] * 2,
                pl.BlockSpec((rows, tile), lambda t, *_: (0, t)),
                pl.BlockSpec((1, tile), lambda t, *_: (0, t)),
            ],
            out_specs=pl.BlockSpec((hidden, 2, rows, tile), lambda t, *_: (0, 0, 0, t)),
            scratch_shapes=[pltpu.VMEM((2, tile // lane, hidden * (rows + 1), lane), f32)],
        ),
        out_shape=pltpu.VMEM((hidden, 2, rows, total), bf16),
        compiler_params=params(32),
        name="project",
    )(
        where,
        residue_mask,
        stay(pair_rep),
        *[stay(w) for w in weights],
        stay(gain),
        stay(bias),
        stay(pair_mask),
        stay(residue_mask[None]),
    )


def gate_kernel(where, x_ref, w0, w1, w2, w3, gain_ref, bias_ref, out_ref, held):
    share, tile, _ = x_ref.shape
    channels = out_ref.shape[0]
    parts = (w0, w1, w2, w3)
    each = channels // len(parts)
    step = share + 1
    gain = widen(column(gain_ref[...]), tile)
    bias = widen(column(bias_ref[...]), tile)
    weights = jnp.concatenate([part[...] for part in parts], 0)
    for i in range(share):
        y = jnp.dot(weights, normed_columns(x_ref[i], gain, bias), preferred_element_type=f32)
        result = 0.5 * jnp.tanh(0.5 * y) + 0.5
        for shift in range(len(parts)):
            owner = lax.rem(where[1] - shift + len(parts), len(parts))
            for part in range(tile // lane):
                held[part, pl.ds(owner * (each * step) + i, each, stride=step), :] = result[
                    shift * each : (shift + 1) * each, part * lane : (part + 1) * lane
                ]
    for part in range(tile // lane):
        for c in range(channels):
            out_ref[c, :, part * lane : (part + 1) * lane] = held[
                part, pl.ds(c * step, share), :
            ].astype(bf16)


def gates(where, pair_rep, weights, gain, bias, share, tile):
    _, total, width = pair_rep.shape
    each = weights[0].shape[0]
    channels = each * len(weights)
    return pl.pallas_call(
        gate_kernel,
        grid_spec=pltpu.PrefetchScalarGridSpec(
            num_scalar_prefetch=1,
            grid=(total // tile,),
            in_specs=[
                pl.BlockSpec((share, tile, width), lambda t, where: (where[1], t, 0)),
                *[pl.BlockSpec((each, width), lambda t, where: (0, 0))] * len(weights),
                *[pl.BlockSpec((1, width), lambda t, where: (0, 0))] * 2,
            ],
            out_specs=pl.BlockSpec((channels, share, tile), lambda t, where: (0, 0, t)),
            scratch_shapes=[pltpu.VMEM((tile // lane, channels * (share + 1), lane), f32)],
        ),
        out_shape=pltpu.HBM((channels, share, total), bf16),
        compiler_params=params(16),
        cost_estimate=pl.CostEstimate(
            flops=2 * share * total * width * channels,
            bytes_accessed=4 * share * total * width,
            transcendentals=share * total * channels,
        ),
        name="gates",
    )(where, stay(pair_rep), *weights, stay(gain), stay(bias))


def product_kernel(left_ref, right_ref, out_ref):
    total = left_ref.shape[-1]
    left = left_ref[...].reshape(-1, total)
    right = right_ref[...].reshape(-1, total)
    out_ref[...] = rows_by_rows(left, right).astype(bf16).reshape(out_ref.shape)


def products(both, share, steps):
    blocks, _, rows, total = both.shape
    tile = blocks // steps
    return pl.pallas_call(
        product_kernel,
        grid=(steps,),
        in_specs=[
            pl.BlockSpec((tile, None, rows, total), lambda t: (t, 0, 0, 0)),
            pl.BlockSpec((blocks, None, rows, total), lambda t: (0, 1, 0, 0)),
        ],
        out_specs=pl.BlockSpec((tile * rows // share, share, total), lambda t: (t, 0, 0)),
        out_shape=jax.ShapeDtypeStruct((blocks * rows // share, share, total), bf16),
        compiler_params=params(20),
        name="products",
    )(both, both)


def update_kernel(p_ref, gate_ref, gain_ref, bias_ref, w_ref, out_ref, spread, gains, biases):
    hidden, share, tile = p_ref.shape
    channels = gate_ref.shape[0]
    span = lane // pack

    @pl.when(pl.program_id(0) == 0)
    def _():
        wide = (hidden, hidden * share)
        source = lax.broadcasted_iota(jnp.int32, wide, 0) * share
        target = lax.broadcasted_iota(jnp.int32, wide, 1)
        repeat = jnp.logical_and(target >= source, target < source + share)
        along = jnp.dot(w_ref[...], repeat.astype(bf16), preferred_element_type=f32)
        row = lax.broadcasted_iota(jnp.int32, (1, share, hidden * share), 1)
        place = lax.broadcasted_iota(jnp.int32, (1, share, hidden * share), 2)
        own = (lax.rem(place, share) == row).astype(f32)
        spread[...] = (along[:, None, :] * own).reshape(spread.shape).astype(bf16)
        gains[...] = jnp.broadcast_to(column(gain_ref[...])[:, None, :], gains.shape)
        biases[...] = jnp.broadcast_to(column(bias_ref[...])[:, None, :], biases.shape)

    values = p_ref[...].astype(f32)
    mean = jnp.sum(values, axis=0, keepdims=True) * (1.0 / hidden)
    centred = values - mean
    var = jnp.sum(centred * centred, axis=0, keepdims=True) * (1.0 / hidden)
    normed = centred * lax.rsqrt(var + eps) * widen(gains[...], tile) + widen(biases[...], tile)
    normed = normed.reshape(hidden * share, tile).astype(bf16)
    projected = jnp.dot(spread[...], normed, preferred_element_type=f32)
    gate = gate_ref[...].astype(f32).reshape(channels * share, tile)
    result = (gate * projected).reshape(channels // pack, pack, share, tile)
    for block in range(tile // span):
        first = block * span
        piece = jnp.concatenate(
            [result[:, c, :, first : first + span] for c in range(pack)], axis=-1
        )
        out_ref[block] = piece.astype(bf16).reshape(out_ref.shape[1:])


def updates(product, gating, gain, bias, weights, tile):
    hidden, share, total = product.shape
    channels = gating.shape[0]
    span = lane // pack
    rows = channels * share // pack
    return pl.pallas_call(
        update_kernel,
        grid=(total // tile,),
        in_specs=[
            pl.BlockSpec((hidden, share, tile), lambda t: (0, 0, t)),
            pl.BlockSpec((channels, share, tile), lambda t: (0, 0, t)),
            pl.BlockSpec((1, hidden), lambda t: (0, 0)),
            pl.BlockSpec((1, hidden), lambda t: (0, 0)),
            pl.BlockSpec((channels, hidden), lambda t: (0, 0)),
        ],
        out_specs=pl.BlockSpec((tile // span, rows, lane), lambda t: (t, 0, 0)),
        out_shape=jax.ShapeDtypeStruct((total // span, rows, lane), bf16),
        scratch_shapes=[
            pltpu.VMEM((channels * share, hidden * share), bf16),
            pltpu.VMEM((hidden, share, lane), f32),
            pltpu.VMEM((hidden, share, lane), f32),
        ],
        compiler_params=params(28),
        name="updates",
    )(product, stay(gating), stay(gain), stay(bias), weights)


def place_kernel(u_ref, out_ref):
    blocks, rows, lanes = u_ref.shape
    groups = out_ref.shape[0] // pack
    share = rows // groups
    for g in range(groups):
        flat = u_ref[:, g * share : (g + 1) * share, :].astype(f32).reshape(blocks * share, lanes)
        out_ref[pack * g : pack * (g + 1)] = flat.T.astype(bf16).reshape(
            pack, lanes // pack, blocks * share
        )


def place(received, share, each):
    blocks, rows, lanes = received.shape
    groups = rows // share
    shape = (lanes // pack, blocks * share)
    return pl.pallas_call(
        place_kernel,
        grid=(groups // each,),
        in_specs=[pl.BlockSpec((blocks, share * each, lanes), lambda g: (0, g, 0))],
        out_specs=pl.BlockSpec((pack * each, *shape), lambda g: (g, 0, 0)),
        out_shape=jax.ShapeDtypeStruct((groups * pack, *shape), bf16),
        compiler_params=params(20),
        name="place",
    )(received)


def exchange(blocks, axes):
    return lax.all_to_all(blocks, axes, split_axis=0, concat_axis=0, tiled=True)


def from_before(own, axis):
    count = lax.axis_size(axis)
    return [own] + [
        lax.ppermute(own, axis, [(k, (k + shift) % count) for k in range(count)])
        for shift in range(1, count)
    ]


def on_device(
    pair_rep,
    residue_mask,
    pair_mask,
    input_gain,
    input_bias,
    left_proj,
    left_gate,
    right_proj,
    right_gate,
    gate_weight,
    output_gain,
    output_bias,
    out_weight,
):
    rows, total, _ = pair_rep.shape
    parts = lax.axis_size("rep")
    share = rows // parts
    where = jnp.stack([lax.axis_index("dap"), lax.axis_index("rep")]).astype(jnp.int32)
    gain_in, bias_in = input_gain[None], input_bias[None]
    all_gates = from_before(gate_weight.T, "rep")
    both = project(
        where,
        residue_mask,
        pair_rep,
        [left_proj.T, left_gate.T, right_proj.T, right_gate.T],
        gain_in,
        bias_in,
        pair_mask,
        256,
    )
    both, all_gates = lax.optimization_barrier((both, all_gates))
    both = exchange(both, "dap")
    both, all_gates = lax.optimization_barrier((both, all_gates))
    gating = gates(where, pair_rep, all_gates, gain_in, bias_in, share, 256)

    def arrival(values):
        per = values.shape[0] // parts
        return jnp.swapaxes(values.reshape(parts, per, *values.shape[1:]), 0, 1).reshape(
            values.shape
        )

    product = exchange(products(both, share, 2), everyone)
    update = updates(
        product,
        gating,
        arrival(output_gain)[None],
        arrival(output_bias)[None],
        arrival(out_weight).T,
        256,
    )
    update = exchange(update.reshape(total // share, -1, lane), everyone)
    return jnp.swapaxes(place(update, share, 4), 1, 2)


def solution(mesh):
    in_specs = (
        P("dap", None, None),
        P(),
        P("dap", None),
        P(),
        P(),
        P(None, "rep"),
        P(None, "rep"),
        P(None, "rep"),
        P(None, "rep"),
        P(None, "rep"),
        P(),
        P(),
        P(),
    )
    out_specs = P("rep", None, "dap")
    return jax.shard_map(
        on_device, mesh=mesh, in_specs=in_specs, out_specs=out_specs, check_vma=False
    )
```

time: 1050 us -> 159 us (0.15)
  waiting for transfers between devices: 753 us -> 21.7 us
  local copies, waits for them, and re-layouts: 151 us -> 1.86 us
  blocking collectives: 30.5 us -> 90.9 us
  matrix products: 50.8 us -> 0 us
  other arithmetic: 41.8 us -> 0.07 us
  Pallas kernels: 0 us -> 30.4 us
  between operations: 14 us -> 0.09 us
    all_gather x2 -> x0, waiting for transfers between devices: 717 us -> none  [the longest x1 717 us: on_device(): lax.all_gather(right, 'dap', axis=1, tiled=True)]
    unnamed x42 -> x8, local copies, waits for them, and re-layouts: 62.5 us -> 0.01 us
    all_to_all x1 -> x2, blocking collectives: 30.5 us -> 90.9 us  [exchange(): return lax.all_to_all(blocks, axes, split_axis=0, concat_axis=0, tiled=True)]
    convert_element_type x5 -> x0, local copies, waits for them, and re-layouts: 59.9 us -> none  [the longest x3 35.2 us: on_device(): return (gate_cols.astype(jnp.float32) * projected).astype(jnp.bfloat16)]
    dot_general x7 -> x0, matrix products: 50.8 us -> none  [the longest x1 28.2 us: on_device(): jnp.einsum('cik,cjk->cij', left, lax.all_gather(right, 'dap', axis=1, til...]
    pallas_call x0 -> x5, Pallas kernels: none -> 30.4 us  [the longest x1 10.9 us: project(): pl.pallas_call(project_kernel, grid_spec=pltpu.PrefetchScalarGridSpec(num...]
    all_to_all x2 -> x0, local copies, waits for them, and re-layouts: 28.9 us -> none  [on_device(): lax.all_to_all(product, 'dap', split_axis=2, concat_axis=1, tiled=True)]
    reduce_sum x4 -> x0, other arithmetic: 25.3 us -> none  [the longest x1 11 us: on_device(): var_in = jnp.mean(centred_in * centred_in, axis=-1, keepdims=True)]
  transfers between devices with their start and end apart: 3 -> 4, of which waited for: 2 -> 1; matrix products, arithmetic and copies ran while one was open for 8% -> 1% of each run, Pallas kernels for 0% -> 11%
where the time goes in v2:
time: 159 us
  blocking collectives  90.9 us (57%)
  Pallas kernels  30.4 us (19%)
  waiting for transfers between devices  21.7 us (14%)
  starting transfers between devices  14.1 us (9%)
  local copies, waits for them, and re-layouts  1.86 us (1%)
    all_to_all x2, blocking collectives, exchange(): return lax.all_to_all(blocks, axes, split_axis=0, concat_axis=0, tiled=True)  90.9 us
    all_to_all x1, waiting for transfers between devices, exchange(): return lax.all_to_all(blocks, axes, split_axis=0, concat_axis=0, tiled=True)  21.7 us
    pallas_call x1, Pallas kernels, project(): pl.pallas_call(project_kernel, grid_spec=pltpu.PrefetchScalarGridSpec(num...  10.9 us
    all_to_all x1, starting transfers between devices, exchange(): return lax.all_to_all(blocks, axes, split_axis=0, concat_axis=0, tiled=True)  9.49 us
    pallas_call x1, Pallas kernels, updates(): pl.pallas_call(update_kernel, grid=(total // tile,), in_specs=[pl.BlockSp...  7.36 us
    pallas_call x1, Pallas kernels, gates(): pl.pallas_call(gate_kernel, grid_spec=pltpu.PrefetchScalarGridSpec(num_sc...  6.45 us
    ppermute x3, starting transfers between devices, from_before(): lax.ppermute(own, axis, [(k, (k + shift) % count) for k in range(count)])  4.56 us
    pallas_call x1, Pallas kernels, products(): pl.pallas_call(product_kernel, grid=(steps,), in_specs=[pl.BlockSpec((til...  3.85 us
  transfers between devices with their start and end apart: 4, of which 1 were waited for; matrix products, arithmetic and copies ran while one was open for 1% of the time, Pallas kernels for 11%

profile of v2, /device:TPU:1, one launch (start us, length us, event | category | flops | bytes accessed | tf_op | source)
XLA Modules:
  0.0 159.1 jit_solution(8769024200332789258)
XLA Ops:
  0.0 4.1 %collective-permute-start = (bf16[32,128]{1,0:T(8,128)(2,1)}, bf16[32,128]{1,0:T(8,128)(2,1)S(1)}, u32[]{:S(2)}, u32[]{:S(2)}) collective-permute-start(bf16[32,128]{1,0:T(8,128)(2,1)} %bitcast.21), channel_id=1, source_target_pairs={{0,1},{1,2},{2,3},{3,0},{4,5},{5,6},{6,7},{7,4},{8,9},{9,10},{10,1... | collective-permute-start | bytes 24584 | tf_op jit(solution)/shard_map/ppermute | solution.py:304
  4.1 0.1 collective-permute-start.1
  4.3 0.3 collective-permute-start.2
  4.6 0.1 pad_add_fusion.where
  4.6 10.9 %project.1 = bf16[32,2,32,1024]{3,2,1,0:T(8,128)(2,1)S(1)} custom-call(s32[2]{0:T(128)S(1)} %pad_add_fusion.where, s32[1024]{0:T(1024)} %residues.1, bf16[32,1024,128]{2,1,0:T(8,128)(2,1)} %x_ref.3, bf16[32,128]{1,0:T(8,128)(2,1)} %bitcast.30, bf16[32,128]{1,0:T(8,128)(2,1)} %bitcast.31, bf16[32,128]{1,0:T(8,128)(2,1)} %bitcast.32, ...), custom_call_target="tpu_custom_call" | custom-call | tf_op jit(solution)/shard_map/project/pallas_call | solution.py:101
  15.6 0.0 collective-permute-done.w1
  15.6 0.0 collective-permute-done.1.w2
  15.6 0.0 collective-permute-done.2.w3
  15.6 56.2 %all_to_all.15.left_ref.right_ref = bf16[32,2,32,1024]{3,2,1,0:T(8,128)(2,1)S(1)} all-to-all(bf16[32,2,32,1024]{3,2,1,0:T(8,128)(2,1)S(1)} %project.1), channel_id=1, replica_groups=mesh['dap'=32,'rep'=4] {'dap'}, dimensions={0} | all-to-all | bytes 8388608 | tf_op jit(solution)/shard_map/all_to_all | solution.py:298
  71.8 3.8 %products.1 = bf16[128,8,1024]{2,1,0:T(8,128)(2,1)} custom-call(bf16[32,2,32,1024]{3,2,1,0:T(8,128)(2,1)S(1)} %all_to_all.15.left_ref.right_ref, bf16[32,2,32,1024]{3,2,1,0:T(8,128)(2,1)S(1)} %all_to_all.15.left_ref.right_ref), custom_call_target="tpu_custom_call" | custom-call | tf_op jit(solution)/shard_map/products/pallas_call | solution.py:194
  75.7 9.5 %all-to-all-start.1 = ((bf16[128,8,1024]{2,1,0:T(8,128)(2,1)}), bf16[128,8,1024]{2,1,0:T(8,128)(2,1)S(1)}, u32[]{:S(2)}, u32[]{:S(2)}) async-start(bf16[128,8,1024]{2,1,0:T(8,128)(2,1)} %products.1), calls=%async_computation.1 | async-start | bytes 4194304 | tf_op jit(solution)/shard_map/all_to_all | solution.py:298
  85.2 0.1 copy.20
  85.4 0.0 copy-done.2
  85.4 0.1 reshape.15
  85.4 0.1 copy.17
  85.5 0.7 broadcast_in_dim_reshape.6.gain_ref
  86.2 0.1 reshape.16
  86.3 0.1 copy.18
  86.4 0.7 broadcast_in_dim_reshape.7.bias_ref
  87.1 6.5 %gates.1.gate_ref = bf16[128,8,1024]{2,1,0:T(8,128)(2,1)} custom-call(s32[2]{0:T(128)S(1)} %pad_add_fusion.where, bf16[32,1024,128]{2,1,0:T(8,128)(2,1)} %x_ref.3, bf16[32,128]{1,0:T(8,128)(2,1)S(1)} %bitcast.24, bf16[32,128]{1,0:T(8,128)(2,1)S(1)} %collective-permute-done.w1, bf16[32,128]{1,0:T(8,128)(2,1)S(1)} %collective-permute-done.1.w2, ...), custom_call_target="tpu_custom_call" | custom-call | flops 268435456 | bytes 4194304 | tf_op jit(solution)/shard_map/gates/pallas_call | solution.py:160
  93.5 21.7 %all-to-all-done.1.p_ref = bf16[128,8,1024]{2,1,0:T(8,128)(2,1)S(1)} async-done(((bf16[128,8,1024]{2,1,0:T(8,128)(2,1)}), bf16[128,8,1024]{2,1,0:T(8,128)(2,1)S(1)}, u32[]{:S(2)}, u32[]{:S(2)}) %all-to-all-start.1) | async-done | bytes 2097184 | tf_op jit(solution)/shard_map/all_to_all | solution.py:298
  115.2 7.4 %updates.1 = bf16[32,256,128]{2,1,0:T(8,128)(2,1)S(1)} custom-call(bf16[128,8,1024]{2,1,0:T(8,128)(2,1)S(1)} %all-to-all-done.1.p_ref, bf16[128,8,1024]{2,1,0:T(8,128)(2,1)} %gates.1.gate_ref, f32[1,128]{1,0:T(1,128)} %broadcast_in_dim_reshape.6.gain_ref, f32[1,128]{1,0:T(1,128)} %broadcast_in_dim_reshape.7.bias_ref, bf16[128,128]{1,0:T(8,128)(2,1)S(1)} %bitcast.20), custom_call_target="tpu_custom_call" | custom-call | tf_op jit(solution)/shard_map/updates/pallas_call | solution.py:249
  122.6 34.6 %all_to_all.16.u_ref = bf16[128,64,128]{2,1,0:T(8,128)(2,1)S(1)} all-to-all(bf16[128,64,128]{2,1,0:T(8,128)(2,1)S(1)} %bitcast.19), channel_id=1, replica_groups=mesh['dap'=32,'rep'=4] {'dap','rep'}, dimensions={0} | all-to-all | bytes 4194304 | tf_op jit(solution)/shard_map/all_to_all | solution.py:298
  157.2 1.8 %place.1 = bf16[32,32,1024]{2,1,0:T(8,128)(2,1)} custom-call(bf16[128,64,128]{2,1,0:T(8,128)(2,1)S(1)} %all_to_all.16.u_ref), custom_call_target="tpu_custom_call" | custom-call | tf_op jit(solution)/shard_map/place/pallas_call | solution.py:286
  (8 shorter events, 0.0 us)
Async XLA Ops:
  0.0 15.6 %collective-permute-start = (bf16[32,128]{1,0:T(8,128)(2,1)}, bf16[32,128]{1,0:T(8,128)(2,1)S(1)}, u32[]{:S(2)}, u32[]{:S(2)}) collective-permute-start(bf16[32,128]{1,0:T(8,128)(2,1)} %bitcast.21), channel_id=1, source_target_pairs={{0,1},{1,2},{2,3},{3,0},{4,5},{5,6},{6,7},{7,4},{8,9},{9,10},{10,1... | collective-permute-start | bytes 24584 | tf_op jit(solution)/shard_map/ppermute | solution.py:304
  4.1 11.5 %collective-permute-start.1 = (bf16[32,128]{1,0:T(8,128)(2,1)}, bf16[32,128]{1,0:T(8,128)(2,1)S(1)}, u32[]{:S(2)}, u32[]{:S(2)}) collective-permute-start(bf16[32,128]{1,0:T(8,128)(2,1)} %bitcast.22), channel_id=1, source_target_pairs={{0,2},{1,3},{2,0},{3,1},{4,6},{5,7},{6,4},{7,5},{8,10},{9,11},{10,... | collective-permute-start | bytes 24584 | tf_op jit(solution)/shard_map/ppermute | solution.py:304
  4.3 11.3 %collective-permute-start.2 = (bf16[32,128]{1,0:T(8,128)(2,1)}, bf16[32,128]{1,0:T(8,128)(2,1)S(1)}, u32[]{:S(2)}, u32[]{:S(2)}) collective-permute-start(bf16[32,128]{1,0:T(8,128)(2,1)} %bitcast.23), channel_id=1, source_target_pairs={{0,3},{1,0},{2,1},{3,2},{4,7},{5,4},{6,5},{7,6},{8,11},{9,8},{10,9... | collective-permute-start | bytes 24584 | tf_op jit(solution)/shard_map/ppermute | solution.py:304
  75.7 9.5 %copy-start.1 = (bf16[128,128]{1,0:T(8,128)(2,1)S(1)}, bf16[128,128]{1,0:T(8,128)(2,1)}, u32[]{:S(2)}) copy-start(bf16[128,128]{1,0:T(8,128)(2,1)} %param.25) | copy-start | bytes 98308
  75.7 9.7 %copy-start.2 = (f32[128]{0:T(128)S(1)}, f32[128]{0:T(128)}, u32[]{:S(2)}) copy-start(f32[128]{0:T(128)} %param.23) | copy-start | bytes 1540
  75.7 10.5 %copy-start.3 = (f32[128]{0:T(128)S(1)}, f32[128]{0:T(128)}, u32[]{:S(2)}) copy-start(f32[128]{0:T(128)} %param.24) | copy-start | bytes 1540
  75.7 11.4 %copy-start = (bf16[128,32]{0,1:T(8,128)(2,1)S(1)}, bf16[128,32]{0,1:T(8,128)(2,1)}, u32[]{:S(2)}) copy-start(bf16[128,32]{0,1:T(8,128)(2,1)} %param.22) | copy-start | bytes 24580
  75.7 39.5 %all-to-all-start.1 = ((bf16[128,8,1024]{2,1,0:T(8,128)(2,1)}), bf16[128,8,1024]{2,1,0:T(8,128)(2,1)S(1)}, u32[]{:S(2)}, u32[]{:S(2)}) async-start(bf16[128,8,1024]{2,1,0:T(8,128)(2,1)} %products.1), calls=%async_computation.1 | async-start | bytes 4194304 | tf_op jit(solution)/shard_map/all_to_all | solution.py:298

commit v3 on v2

--- a/solution.py
+++ b/solution.py
@@ -1,3 +1,5 @@
+import functools
+
 import jax
 import jax.numpy as jnp
 from jax import lax
@@ -19,6 +21,13 @@
 
 def stay(array):
     return pltpu.with_memory_space_constraint(array, pltpu.HBM)
+
+
+def near(array):
+    return pltpu.with_memory_space_constraint(array, pltpu.VMEM)
+
+
+whole = pl.BlockSpec(memory_space=pltpu.VMEM)
 
 
 def rows_by_rows(a, b):
@@ -64,6 +73,7 @@
     rows, tile, width = x_ref.shape
     hidden = out_ref.shape[0]
     step = rows + 1
+    begin = pl.program_id(0) * tile
     weights = jnp.concatenate(
         [left_proj[...], left_gate[...], right_proj[...], right_gate[...]], 0
     )
@@ -86,9 +96,10 @@
     for side in range(2):
         for part in range(tile // lane):
             for c in range(hidden):
-                out_ref[c, side, :, part * lane : (part + 1) * lane] = held[
-                    side, part, pl.ds(c * step, rows), :
-                ].astype(bf16)
+                across = pl.ds(pl.multiple_of(begin + part * lane, lane), lane)
+                out_ref[c, side, :, across] = held[side, part, pl.ds(c * step, rows), :].astype(
+                    bf16
+                )
 
 
 def project(where, residue_mask, pair_rep, weights, gain, bias, pair_mask, tile):
@@ -110,7 +121,7 @@
                 pl.BlockSpec((rows, tile), lambda t, *_: (0, t)),
                 pl.BlockSpec((1, tile), lambda t, *_: (0, t)),
             ],
-            out_specs=pl.BlockSpec((hidden, 2, rows, tile), lambda t, *_: (0, 0, 0, t)),
+            out_specs=whole,
             scratch_shapes=[pltpu.VMEM((2, tile // lane, hidden * (rows + 1), lane), f32)],
         ),
         out_shape=pltpu.VMEM((hidden, 2, rows, total), bf16),
@@ -167,10 +178,10 @@
                 *[pl.BlockSpec((each, width), lambda t, where: (0, 0))] * len(weights),
                 *[pl.BlockSpec((1, width), lambda t, where: (0, 0))] * 2,
             ],
-            out_specs=pl.BlockSpec((channels, share, tile), lambda t, where: (0, 0, t)),
+            out_specs=pl.BlockSpec((None, channels, share, tile), lambda t, where: (t, 0, 0, 0)),
             scratch_shapes=[pltpu.VMEM((tile // lane, channels * (share + 1), lane), f32)],
         ),
-        out_shape=pltpu.HBM((channels, share, total), bf16),
+        out_shape=pltpu.HBM((total // tile, channels, share, tile), bf16),
         compiler_params=params(16),
         cost_estimate=pl.CostEstimate(
             flops=2 * share * total * width * channels,
@@ -181,91 +192,94 @@
     )(where, stay(pair_rep), *weights, stay(gain), stay(bias))
 
 
-def product_kernel(left_ref, right_ref, out_ref):
-    total = left_ref.shape[-1]
-    left = left_ref[...].reshape(-1, total)
-    right = right_ref[...].reshape(-1, total)
+def product_kernel(both_ref, out_ref):
+    blocks, _, rows, total = both_ref.shape
+    tile = out_ref.shape[0] * out_ref.shape[1] // rows
+    left = both_ref[pl.ds(pl.program_id(0) * tile, tile), 0].reshape(-1, total)
+    right = both_ref[:, 1].reshape(-1, total)
     out_ref[...] = rows_by_rows(left, right).astype(bf16).reshape(out_ref.shape)
 
 
 def products(both, share, steps):
     blocks, _, rows, total = both.shape
-    tile = blocks // steps
+    count = blocks * rows // share
     return pl.pallas_call(
         product_kernel,
         grid=(steps,),
-        in_specs=[
-            pl.BlockSpec((tile, None, rows, total), lambda t: (t, 0, 0, 0)),
-            pl.BlockSpec((blocks, None, rows, total), lambda t: (0, 1, 0, 0)),
-        ],
-        out_specs=pl.BlockSpec((tile * rows // share, share, total), lambda t: (t, 0, 0)),
-        out_shape=jax.ShapeDtypeStruct((blocks * rows // share, share, total), bf16),
+        in_specs=[whole],
+        out_specs=pl.BlockSpec((count // steps, share, total), lambda t: (t, 0, 0)),
+        out_shape=pltpu.HBM((count, share, total), bf16),
         compiler_params=params(20),
         name="products",
-    )(both, both)
-
-
-def update_kernel(p_ref, gate_ref, gain_ref, bias_ref, w_ref, out_ref, spread, gains, biases):
-    hidden, share, tile = p_ref.shape
-    channels = gate_ref.shape[0]
+    )(near(both))
+
+
+def update_kernel(
+    p_ref, gate_hbm, gain_ref, bias_ref, w_ref, out_ref, gate_ref, spread, gains, biases, sems, *, tile
+):
+    hidden, share, total = p_ref.shape
+    channels = gate_ref.shape[1]
     span = lane // pack
-
-    @pl.when(pl.program_id(0) == 0)
-    def _():
-        wide = (hidden, hidden * share)
-        source = lax.broadcasted_iota(jnp.int32, wide, 0) * share
-        target = lax.broadcasted_iota(jnp.int32, wide, 1)
-        repeat = jnp.logical_and(target >= source, target < source + share)
-        along = jnp.dot(w_ref[...], repeat.astype(bf16), preferred_element_type=f32)
-        row = lax.broadcasted_iota(jnp.int32, (1, share, hidden * share), 1)
-        place = lax.broadcasted_iota(jnp.int32, (1, share, hidden * share), 2)
-        own = (lax.rem(place, share) == row).astype(f32)
-        spread[...] = (along[:, None, :] * own).reshape(spread.shape).astype(bf16)
-        gains[...] = jnp.broadcast_to(column(gain_ref[...])[:, None, :], gains.shape)
-        biases[...] = jnp.broadcast_to(column(bias_ref[...])[:, None, :], biases.shape)
-
-    values = p_ref[...].astype(f32)
-    mean = jnp.sum(values, axis=0, keepdims=True) * (1.0 / hidden)
-    centred = values - mean
-    var = jnp.sum(centred * centred, axis=0, keepdims=True) * (1.0 / hidden)
-    normed = centred * lax.rsqrt(var + eps) * widen(gains[...], tile) + widen(biases[...], tile)
-    normed = normed.reshape(hidden * share, tile).astype(bf16)
-    projected = jnp.dot(spread[...], normed, preferred_element_type=f32)
-    gate = gate_ref[...].astype(f32).reshape(channels * share, tile)
-    result = (gate * projected).reshape(channels // pack, pack, share, tile)
-    for block in range(tile // span):
-        first = block * span
-        piece = jnp.concatenate(
-            [result[:, c, :, first : first + span] for c in range(pack)], axis=-1
+    starts = range(0, total, tile)
+    copies = [
+        pltpu.make_async_copy(gate_hbm.at[number], gate_ref.at[number], sems.at[number])
+        for number in range(len(starts))
+    ]
+    for copy in copies:
+        copy.start()
+    wide = (hidden, hidden * share)
+    source = lax.broadcasted_iota(jnp.int32, wide, 0) * share
+    target = lax.broadcasted_iota(jnp.int32, wide, 1)
+    repeat = jnp.logical_and(target >= source, target < source + share)
+    along = jnp.dot(w_ref[...], repeat.astype(bf16), preferred_element_type=f32)
+    row = lax.broadcasted_iota(jnp.int32, (1, share, hidden * share), 1)
+    place = lax.broadcasted_iota(jnp.int32, (1, share, hidden * share), 2)
+    own = (lax.rem(place, share) == row).astype(f32)
+    spread[...] = (along[:, None, :] * own).reshape(spread.shape).astype(bf16)
+    gains[...] = jnp.broadcast_to(column(gain_ref[...])[:, None, :], gains.shape)
+    biases[...] = jnp.broadcast_to(column(bias_ref[...])[:, None, :], biases.shape)
+    for number, begin in enumerate(starts):
+        across = slice(begin, begin + tile)
+        values = p_ref[:, :, across].astype(f32)
+        mean = jnp.sum(values, axis=0, keepdims=True) * (1.0 / hidden)
+        centred = values - mean
+        var = jnp.sum(centred * centred, axis=0, keepdims=True) * (1.0 / hidden)
+        normed = centred * lax.rsqrt(var + eps) * widen(gains[...], tile) + widen(
+            biases[...], tile
         )
-        out_ref[block] = piece.astype(bf16).reshape(out_ref.shape[1:])
+        normed = normed.reshape(hidden * share, tile).astype(bf16)
+        projected = jnp.dot(spread[...], normed, preferred_element_type=f32)
+        if number == 0:
+            for copy in copies:
+                copy.wait()
+        gate = gate_ref[number].astype(f32).reshape(channels * share, tile)
+        result = (gate * projected).reshape(channels // pack, pack, share, tile)
+        for first in range(0, tile, span):
+            piece = jnp.concatenate(
+                [result[:, c, :, first : first + span] for c in range(pack)], axis=-1
+            )
+            out_ref[(begin + first) // span] = piece.astype(bf16).reshape(out_ref.shape[1:])
 
 
 def updates(product, gating, gain, bias, weights, tile):
     hidden, share, total = product.shape
-    channels = gating.shape[0]
+    channels = gating.shape[1]
     span = lane // pack
-    rows = channels * share // pack
-    return pl.pallas_call(
-        update_kernel,
-        grid=(total // tile,),
-        in_specs=[
-            pl.BlockSpec((hidden, share, tile), lambda t: (0, 0, t)),
-            pl.BlockSpec((channels, share, tile), lambda t: (0, 0, t)),
-            pl.BlockSpec((1, hidden), lambda t: (0, 0)),
-            pl.BlockSpec((1, hidden), lambda t: (0, 0)),
-            pl.BlockSpec((channels, hidden), lambda t: (0, 0)),
-        ],
-        out_specs=pl.BlockSpec((tile // span, rows, lane), lambda t: (t, 0, 0)),
-        out_shape=jax.ShapeDtypeStruct((total // span, rows, lane), bf16),
+    return pl.pallas_call(
+        functools.partial(update_kernel, tile=tile),
+        in_specs=[whole, pl.BlockSpec(memory_space=pltpu.HBM), whole, whole, whole],
+        out_specs=whole,
+        out_shape=pltpu.VMEM((total // span, channels * share // pack, lane), bf16),
         scratch_shapes=[
+            pltpu.VMEM(gating.shape, bf16),
             pltpu.VMEM((channels * share, hidden * share), bf16),
             pltpu.VMEM((hidden, share, lane), f32),
             pltpu.VMEM((hidden, share, lane), f32),
+            pltpu.SemaphoreType.DMA((total // tile,)),
         ],
         compiler_params=params(28),
         name="updates",
-    )(product, stay(gating), stay(gain), stay(bias), weights)
+    )(near(product), stay(gating), gain, bias, weights)
 
 
 def place_kernel(u_ref, out_ref):
@@ -300,10 +314,11 @@
 
 def from_before(own, axis):
     count = lax.axis_size(axis)
-    return [own] + [
+    parts = [
         lax.ppermute(own, axis, [(k, (k + shift) % count) for k in range(count)])
-        for shift in range(1, count)
+        for shift in range(count - 1, 0, -1)
     ]
+    return [own] + parts[::-1]
 
 
 def on_device(
@@ -339,7 +354,7 @@
     )
     both, all_gates = lax.optimization_barrier((both, all_gates))
     both = exchange(both, "dap")
-    both, all_gates = lax.optimization_barrier((both, all_gates))
+    both, all_gates, out_weight = lax.optimization_barrier((both, all_gates, out_weight))
     gating = gates(where, pair_rep, all_gates, gain_in, bias_in, share, 256)
 
     def arrival(values):

time: 159 us -> 157 us (0.987)
  Pallas kernels: 30.4 us -> 27.9 us
    pallas_call x2, Pallas kernels: 11.2 us -> 8.92 us  [the longest x1 5.37 us: updates(): pl.pallas_call(functools.partial(update_kernel, tile=tile), in_specs=[who...]
  transfers between devices with their start and end apart: 4 -> 4, of which waited for: 1 -> 1; matrix products, arithmetic and copies ran while one was open for 1% -> 0% of each run, Pallas kernels for 11% -> 11%
where the time goes in v3:
time: 157 us
  blocking collectives  90.9 us (58%)
  Pallas kernels  27.9 us (18%)
  waiting for transfers between devices  22.9 us (15%)
  starting transfers between devices  14.1 us (9%)
    all_to_all x2, blocking collectives, exchange(): return lax.all_to_all(blocks, axes, split_axis=0, concat_axis=0, tiled=True)  90.9 us
    all_to_all x1, waiting for transfers between devices, exchange(): return lax.all_to_all(blocks, axes, split_axis=0, concat_axis=0, tiled=True)  22.9 us
    pallas_call x1, Pallas kernels, project(): pl.pallas_call(project_kernel, grid_spec=pltpu.PrefetchScalarGridSpec(num...  10.7 us
    all_to_all x1, starting transfers between devices, exchange(): return lax.all_to_all(blocks, axes, split_axis=0, concat_axis=0, tiled=True)  9.49 us
    pallas_call x1, Pallas kernels, gates(): pl.pallas_call(gate_kernel, grid_spec=pltpu.PrefetchScalarGridSpec(num_sc...  6.41 us
    pallas_call x1, Pallas kernels, updates(): pl.pallas_call(functools.partial(update_kernel, tile=tile), in_specs=[who...  5.37 us
    ppermute x3, starting transfers between devices, from_before(): lax.ppermute(own, axis, [(k, (k + shift) % count) for k in range(count)])  4.56 us
    pallas_call x1, Pallas kernels, products(): pl.pallas_call(product_kernel, grid=(steps,), in_specs=[whole], out_specs...  3.55 us
  transfers between devices with their start and end apart: 4, of which 1 were waited for; matrix products, arithmetic and copies ran while one was open for 0% of the time, Pallas kernels for 11%

profile of v3, /device:TPU:1, one launch (start us, length us, event | category | flops | bytes accessed | tf_op | source)
XLA Modules:
  0.0 156.6 jit_solution(8701994577306904441)
XLA Ops:
  0.0 4.1 %collective-permute-start = (bf16[32,128]{1,0:T(8,128)(2,1)}, bf16[32,128]{1,0:T(8,128)(2,1)S(1)}, u32[]{:S(2)}, u32[]{:S(2)}) collective-permute-start(bf16[32,128]{1,0:T(8,128)(2,1)} %bitcast.21), channel_id=1, source_target_pairs={{0,1},{1,2},{2,3},{3,0},{4,5},{5,6},{6,7},{7,4},{8,9},{9,10},{10,1... | collective-permute-start | bytes 24584 | tf_op jit(solution)/shard_map/ppermute | solution.py:318
  4.1 0.1 collective-permute-start.1
  4.3 0.3 collective-permute-start.2
  4.6 0.1 pad_add_fusion.where
  4.6 10.7 %project.1 = bf16[32,2,32,1024]{3,2,1,0:T(8,128)(2,1)S(1)} custom-call(s32[2]{0:T(128)S(1)} %pad_add_fusion.where, s32[1024]{0:T(1024)} %residues.1, bf16[32,1024,128]{2,1,0:T(8,128)(2,1)} %x_ref.3, bf16[32,128]{1,0:T(8,128)(2,1)} %bitcast.30, bf16[32,128]{1,0:T(8,128)(2,1)} %bitcast.31, bf16[32,128]{1,0:T(8,128)(2,1)} %bitcast.32, ...), custom_call_target="tpu_custom_call" | custom-call | tf_op jit(solution)/shard_map/project/pallas_call | solution.py:112
  15.4 0.0 collective-permute-done.w1
  15.4 0.0 collective-permute-done.1.w2
  15.4 0.0 collective-permute-done.2.w3
  15.4 56.2 %all_to_all.15.both_ref = bf16[32,2,32,1024]{3,2,1,0:T(8,128)(2,1)S(1)} all-to-all(bf16[32,2,32,1024]{3,2,1,0:T(8,128)(2,1)S(1)} %project.1), channel_id=1, replica_groups=mesh['dap'=32,'rep'=4] {'dap'}, dimensions={0} | all-to-all | bytes 8388608 | tf_op jit(solution)/shard_map/all_to_all | solution.py:312
  71.6 3.6 %products.1 = bf16[128,8,1024]{2,1,0:T(8,128)(2,1)} custom-call(bf16[32,2,32,1024]{3,2,1,0:T(8,128)(2,1)S(1)} %all_to_all.15.both_ref), custom_call_target="tpu_custom_call" | custom-call | tf_op jit(solution)/shard_map/products/pallas_call | solution.py:206
  75.2 9.5 %all-to-all-start.1 = ((bf16[128,8,1024]{2,1,0:T(8,128)(2,1)}), bf16[128,8,1024]{2,1,0:T(8,128)(2,1)S(1)}, u32[]{:S(2)}, u32[]{:S(2)}) async-start(bf16[128,8,1024]{2,1,0:T(8,128)(2,1)} %products.1), calls=%async_computation.1 | async-start | bytes 4194304 | tf_op jit(solution)/shard_map/all_to_all | solution.py:312
  84.7 0.0 copy-done.2
  84.7 0.1 reshape.15
  84.8 0.1 copy.17
  84.9 0.1 broadcast_in_dim_reshape.6.gain_ref
  85.0 0.1 reshape.16
  85.1 0.1 copy.18
  85.2 0.1 broadcast_in_dim_reshape.7.bias_ref
  85.3 0.1 copy.20
  85.4 6.4 %gates.1.gate_hbm = bf16[4,128,8,256]{3,2,1,0:T(8,128)(2,1)} custom-call(s32[2]{0:T(128)S(1)} %pad_add_fusion.where, bf16[32,1024,128]{2,1,0:T(8,128)(2,1)} %x_ref.3, bf16[32,128]{1,0:T(8,128)(2,1)S(1)} %bitcast.24, bf16[32,128]{1,0:T(8,128)(2,1)S(1)} %collective-permute-done.w1, bf16[32,128]{1,0:T(8,128)(2,1)S(1)} %collective-permute-done.1.w2, ...), custom_call_target="tpu_custom_call" | custom-call | flops 268435456 | bytes 4194304 | tf_op jit(solution)/shard_map/gates/pallas_call | solution.py:171
  91.8 22.9 %all-to-all-done.1.p_ref = bf16[128,8,1024]{2,1,0:T(8,128)(2,1)S(1)} async-done(((bf16[128,8,1024]{2,1,0:T(8,128)(2,1)}), bf16[128,8,1024]{2,1,0:T(8,128)(2,1)S(1)}, u32[]{:S(2)}, u32[]{:S(2)}) %all-to-all-start.1) | async-done | bytes 2097184 | tf_op jit(solution)/shard_map/all_to_all | solution.py:312
  114.7 5.4 %updates.1 = bf16[32,256,128]{2,1,0:T(8,128)(2,1)S(1)} custom-call(bf16[128,8,1024]{2,1,0:T(8,128)(2,1)S(1)} %all-to-all-done.1.p_ref, bf16[4,128,8,256]{3,2,1,0:T(8,128)(2,1)} %gates.1.gate_hbm, f32[1,128]{1,0:T(1,128)S(1)} %broadcast_in_dim_reshape.6.gain_ref, f32[1,128]{1,0:T(1,128)S(1)} %broadcast_in_dim_reshape.7.bias_ref, bf16[128,128]{1,0:T(8,128)(2,1)S(1)} %bitcast.20), custom_call_target="tpu_custom_call" | custom-call | tf_op jit(solution)/shard_map/updates/pallas_call | solution.py:268
  120.1 34.6 %all_to_all.16.u_ref = bf16[128,64,128]{2,1,0:T(8,128)(2,1)S(1)} all-to-all(bf16[128,64,128]{2,1,0:T(8,128)(2,1)S(1)} %bitcast.19), channel_id=1, replica_groups=mesh['dap'=32,'rep'=4] {'dap','rep'}, dimensions={0} | all-to-all | bytes 4194304 | tf_op jit(solution)/shard_map/all_to_all | solution.py:312
  154.7 1.8 %place.1 = bf16[32,32,1024]{2,1,0:T(8,128)(2,1)} custom-call(bf16[128,64,128]{2,1,0:T(8,128)(2,1)S(1)} %all_to_all.16.u_ref), custom_call_target="tpu_custom_call" | custom-call | tf_op jit(solution)/shard_map/place/pallas_call | solution.py:300
  (8 shorter events, 0.0 us)
Async XLA Ops:
  0.0 15.4 %collective-permute-start = (bf16[32,128]{1,0:T(8,128)(2,1)}, bf16[32,128]{1,0:T(8,128)(2,1)S(1)}, u32[]{:S(2)}, u32[]{:S(2)}) collective-permute-start(bf16[32,128]{1,0:T(8,128)(2,1)} %bitcast.21), channel_id=1, source_target_pairs={{0,1},{1,2},{2,3},{3,0},{4,5},{5,6},{6,7},{7,4},{8,9},{9,10},{10,1... | collective-permute-start | bytes 24584 | tf_op jit(solution)/shard_map/ppermute | solution.py:318
  4.1 11.3 %collective-permute-start.1 = (bf16[32,128]{1,0:T(8,128)(2,1)}, bf16[32,128]{1,0:T(8,128)(2,1)S(1)}, u32[]{:S(2)}, u32[]{:S(2)}) collective-permute-start(bf16[32,128]{1,0:T(8,128)(2,1)} %bitcast.22), channel_id=1, source_target_pairs={{0,2},{1,3},{2,0},{3,1},{4,6},{5,7},{6,4},{7,5},{8,10},{9,11},{10,... | collective-permute-start | bytes 24584 | tf_op jit(solution)/shard_map/ppermute | solution.py:318
  4.3 11.1 %collective-permute-start.2 = (bf16[32,128]{1,0:T(8,128)(2,1)}, bf16[32,128]{1,0:T(8,128)(2,1)S(1)}, u32[]{:S(2)}, u32[]{:S(2)}) collective-permute-start(bf16[32,128]{1,0:T(8,128)(2,1)} %bitcast.23), channel_id=1, source_target_pairs={{0,3},{1,0},{2,1},{3,2},{4,7},{5,4},{6,5},{7,6},{8,11},{9,8},{10,9... | collective-permute-start | bytes 24584 | tf_op jit(solution)/shard_map/ppermute | solution.py:318
  75.2 9.5 %copy-start.2 = (f32[128]{0:T(128)S(1)}, f32[128]{0:T(128)}, u32[]{:S(2)}) copy-start(f32[128]{0:T(128)} %param.23) | copy-start | bytes 1540
  75.2 9.8 %copy-start.3 = (f32[128]{0:T(128)S(1)}, f32[128]{0:T(128)}, u32[]{:S(2)}) copy-start(f32[128]{0:T(128)} %param.24) | copy-start | bytes 1540
  75.2 10.1 %copy-start.1 = (bf16[128,128]{1,0:T(8,128)(2,1)S(1)}, bf16[128,128]{1,0:T(8,128)(2,1)}, u32[]{:S(2)}) copy-start(bf16[128,128]{1,0:T(8,128)(2,1)} %param.25) | copy-start | bytes 98308
  75.2 10.2 %copy-start = (bf16[128,32]{0,1:T(8,128)(2,1)S(1)}, bf16[128,32]{0,1:T(8,128)(2,1)}, u32[]{:S(2)}) copy-start(bf16[128,32]{0,1:T(8,128)(2,1)} %param.22) | copy-start | bytes 24580
  75.2 39.5 %all-to-all-start.1 = ((bf16[128,8,1024]{2,1,0:T(8,128)(2,1)}), bf16[128,8,1024]{2,1,0:T(8,128)(2,1)S(1)}, u32[]{:S(2)}, u32[]{:S(2)}) async-start(bf16[128,8,1024]{2,1,0:T(8,128)(2,1)} %products.1), calls=%async_computation.1 | async-start | bytes 4194304 | tf_op jit(solution)/shard_map/all_to_all | solution.py:312

commit v4 on v3

--- a/solution.py
+++ b/solution.py
@@ -192,23 +192,31 @@
     )(where, stay(pair_rep), *weights, stay(gain), stay(bias))
 
 
-def product_kernel(both_ref, out_ref):
+def product_kernel(both_ref, out_hbm, out_ref, sems, *, counts):
     blocks, _, rows, total = both_ref.shape
-    tile = out_ref.shape[0] * out_ref.shape[1] // rows
-    left = both_ref[pl.ds(pl.program_id(0) * tile, tile), 0].reshape(-1, total)
-    right = both_ref[:, 1].reshape(-1, total)
-    out_ref[...] = rows_by_rows(left, right).astype(bf16).reshape(out_ref.shape)
-
-
-def products(both, share, steps):
+    share = out_ref.shape[1]
+    copies, begin = [], 0
+    for number, count in enumerate(counts):
+        left = both_ref[begin : begin + count, 0].reshape(-1, total)
+        right = both_ref[:, 1].reshape(-1, total)
+        at = pl.ds(begin * rows // share, count * rows // share)
+        out_ref[at] = rows_by_rows(left, right).astype(bf16).reshape(-1, share, total)
+        copies.append(pltpu.make_async_copy(out_ref.at[at], out_hbm.at[at], sems.at[number]))
+        copies[-1].start()
+        begin += count
+    for copy in copies:
+        copy.wait()
+
+
+def products(both, share, counts):
     blocks, _, rows, total = both.shape
-    count = blocks * rows // share
+    shape = (blocks * rows // share, share, total)
     return pl.pallas_call(
-        product_kernel,
-        grid=(steps,),
+        functools.partial(product_kernel, counts=counts),
         in_specs=[whole],
-        out_specs=pl.BlockSpec((count // steps, share, total), lambda t: (t, 0, 0)),
-        out_shape=pltpu.HBM((count, share, total), bf16),
+        out_specs=pl.BlockSpec(memory_space=pltpu.HBM),
+        out_shape=pltpu.HBM(shape, bf16),
+        scratch_shapes=[pltpu.VMEM(shape, bf16), pltpu.SemaphoreType.DMA((len(counts),))],
         compiler_params=params(20),
         name="products",
     )(near(both))
@@ -238,9 +246,9 @@
     spread[...] = (along[:, None, :] * own).reshape(spread.shape).astype(bf16)
     gains[...] = jnp.broadcast_to(column(gain_ref[...])[:, None, :], gains.shape)
     biases[...] = jnp.broadcast_to(column(bias_ref[...])[:, None, :], biases.shape)
-    for number, begin in enumerate(starts):
-        across = slice(begin, begin + tile)
-        values = p_ref[:, :, across].astype(f32)
+
+    def project_tile(begin):
+        values = p_ref[:, :, begin : begin + tile].astype(f32)
         mean = jnp.sum(values, axis=0, keepdims=True) * (1.0 / hidden)
         centred = values - mean
         var = jnp.sum(centred * centred, axis=0, keepdims=True) * (1.0 / hidden)
@@ -248,17 +256,25 @@
             biases[...], tile
         )
         normed = normed.reshape(hidden * share, tile).astype(bf16)
-        projected = jnp.dot(spread[...], normed, preferred_element_type=f32)
-        if number == 0:
-            for copy in copies:
-                copy.wait()
+        return jnp.dot(spread[...], normed, preferred_element_type=f32)
+
+    def gate_tile(number, projected):
         gate = gate_ref[number].astype(f32).reshape(channels * share, tile)
         result = (gate * projected).reshape(channels // pack, pack, share, tile)
         for first in range(0, tile, span):
             piece = jnp.concatenate(
                 [result[:, c, :, first : first + span] for c in range(pack)], axis=-1
             )
-            out_ref[(begin + first) // span] = piece.astype(bf16).reshape(out_ref.shape[1:])
+            out_ref[(starts[number] + first) // span] = piece.astype(bf16).reshape(
+                out_ref.shape[1:]
+            )
+
+    ahead = min(2, len(starts))
+    early = [project_tile(starts[number]) for number in range(ahead)]
+    for copy in copies:
+        copy.wait()
+    for number in range(len(starts)):
+        gate_tile(number, early[number] if number < ahead else project_tile(starts[number]))
 
 
 def updates(product, gating, gain, bias, weights, tile):
@@ -363,7 +379,7 @@
             values.shape
         )
 
-    product = exchange(products(both, share, 2), everyone)
+    product = exchange(products(both, share, (24, 8)), everyone)
     update = updates(
         product,
         gating,

time: 157 us -> 156 us (level)
  no operation moved by 1% of the time
where the time goes in v4:
time: 156 us
  blocking collectives  90.9 us (58%)
  Pallas kernels  26.8 us (17%)
  waiting for transfers between devices  22.9 us (15%)
  starting transfers between devices  14.1 us (9%)
    all_to_all x2, blocking collectives, exchange(): return lax.all_to_all(blocks, axes, split_axis=0, concat_axis=0, tiled=True)  90.9 us
    all_to_all x1, waiting for transfers between devices, exchange(): return lax.all_to_all(blocks, axes, split_axis=0, concat_axis=0, tiled=True)  22.9 us
    pallas_call x1, Pallas kernels, project(): pl.pallas_call(project_kernel, grid_spec=pltpu.PrefetchScalarGridSpec(num...  10.7 us
    all_to_all x1, starting transfers between devices, exchange(): return lax.all_to_all(blocks, axes, split_axis=0, concat_axis=0, tiled=True)  9.49 us
    pallas_call x1, Pallas kernels, gates(): pl.pallas_call(gate_kernel, grid_spec=pltpu.PrefetchScalarGridSpec(num_sc...  6.41 us
    pallas_call x1, Pallas kernels, updates(): pl.pallas_call(functools.partial(update_kernel, tile=tile), in_specs=[who...  4.69 us
    ppermute x3, starting transfers between devices, from_before(): lax.ppermute(own, axis, [(k, (k + shift) % count) for k in range(count)])  4.56 us
    pallas_call x1, Pallas kernels, products(): pl.pallas_call(functools.partial(product_kernel, counts=counts), in_specs...  3.18 us
  transfers between devices with their start and end apart: 4, of which 1 were waited for; matrix products, arithmetic and copies ran while one was open for 0% of the time, Pallas kernels for 11%

profile of v4, /device:TPU:1, one launch (start us, length us, event | category | flops | bytes accessed | tf_op | source)
XLA Modules:
  0.0 155.6 jit_solution(18145671900105978586)
XLA Ops:
  0.0 4.1 %collective-permute-start = (bf16[32,128]{1,0:T(8,128)(2,1)}, bf16[32,128]{1,0:T(8,128)(2,1)S(1)}, u32[]{:S(2)}, u32[]{:S(2)}) collective-permute-start(bf16[32,128]{1,0:T(8,128)(2,1)} %bitcast.21), channel_id=1, source_target_pairs={{0,1},{1,2},{2,3},{3,0},{4,5},{5,6},{6,7},{7,4},{8,9},{9,10},{10,1... | collective-permute-start | bytes 24584 | tf_op jit(solution)/shard_map/ppermute | solution.py:334
  4.1 0.1 collective-permute-start.1
  4.3 0.3 collective-permute-start.2
  4.6 0.1 pad_add_fusion.where
  4.6 10.7 %project.1 = bf16[32,2,32,1024]{3,2,1,0:T(8,128)(2,1)S(1)} custom-call(s32[2]{0:T(128)S(1)} %pad_add_fusion.where, s32[1024]{0:T(1024)} %residues.1, bf16[32,1024,128]{2,1,0:T(8,128)(2,1)} %x_ref.3, bf16[32,128]{1,0:T(8,128)(2,1)} %bitcast.30, bf16[32,128]{1,0:T(8,128)(2,1)} %bitcast.31, bf16[32,128]{1,0:T(8,128)(2,1)} %bitcast.32, ...), custom_call_target="tpu_custom_call" | custom-call | tf_op jit(solution)/shard_map/project/pallas_call | solution.py:112
  15.4 56.2 %all_to_all.15.both_ref = bf16[32,2,32,1024]{3,2,1,0:T(8,128)(2,1)S(1)} all-to-all(bf16[32,2,32,1024]{3,2,1,0:T(8,128)(2,1)S(1)} %project.1), channel_id=1, replica_groups=mesh['dap'=32,'rep'=4] {'dap'}, dimensions={0} | all-to-all | bytes 8388608 | tf_op jit(solution)/shard_map/all_to_all | solution.py:328
  71.6 3.2 %products.1 = bf16[128,8,1024]{2,1,0:T(8,128)(2,1)} custom-call(bf16[32,2,32,1024]{3,2,1,0:T(8,128)(2,1)S(1)} %all_to_all.15.both_ref), custom_call_target="tpu_custom_call" | custom-call | tf_op jit(solution)/shard_map/products/pallas_call | solution.py:214
  74.8 0.0 copy-start.2
  74.8 0.0 copy-start.3
  74.9 0.0 copy-start.1
  74.9 0.0 copy-start
  74.9 9.5 %all-to-all-start.1 = ((bf16[128,8,1024]{2,1,0:T(8,128)(2,1)}), bf16[128,8,1024]{2,1,0:T(8,128)(2,1)S(1)}, u32[]{:S(2)}, u32[]{:S(2)}) async-start(bf16[128,8,1024]{2,1,0:T(8,128)(2,1)} %products.1), calls=%async_computation.1 | async-start | bytes 4194304 | tf_op jit(solution)/shard_map/all_to_all | solution.py:328
  84.4 0.1 reshape.15
  84.5 0.1 copy.17
  84.6 0.1 broadcast_in_dim_reshape.6.gain_ref
  84.7 0.1 reshape.16
  84.8 0.1 copy.18
  84.8 0.1 broadcast_in_dim_reshape.7.bias_ref
  85.0 0.1 copy.20
  85.1 6.4 %gates.1.gate_hbm = bf16[4,128,8,256]{3,2,1,0:T(8,128)(2,1)} custom-call(s32[2]{0:T(128)S(1)} %pad_add_fusion.where, bf16[32,1024,128]{2,1,0:T(8,128)(2,1)} %x_ref.3, bf16[32,128]{1,0:T(8,128)(2,1)S(1)} %bitcast.24, bf16[32,128]{1,0:T(8,128)(2,1)S(1)} %collective-permute-done.w1, bf16[32,128]{1,0:T(8,128)(2,1)S(1)} %collective-permute-done.1.w2, ...), custom_call_target="tpu_custom_call" | custom-call | flops 268435456 | bytes 4194304 | tf_op jit(solution)/shard_map/gates/pallas_call | solution.py:171
  91.5 22.9 %all-to-all-done.1.p_ref = bf16[128,8,1024]{2,1,0:T(8,128)(2,1)S(1)} async-done(((bf16[128,8,1024]{2,1,0:T(8,128)(2,1)}), bf16[128,8,1024]{2,1,0:T(8,128)(2,1)S(1)}, u32[]{:S(2)}, u32[]{:S(2)}) %all-to-all-start.1) | async-done | bytes 2097184 | tf_op jit(solution)/shard_map/all_to_all | solution.py:328
  114.4 4.7 %updates.1 = bf16[32,256,128]{2,1,0:T(8,128)(2,1)S(1)} custom-call(bf16[128,8,1024]{2,1,0:T(8,128)(2,1)S(1)} %all-to-all-done.1.p_ref, bf16[4,128,8,256]{3,2,1,0:T(8,128)(2,1)} %gates.1.gate_hbm, f32[1,128]{1,0:T(1,128)S(1)} %broadcast_in_dim_reshape.6.gain_ref, f32[1,128]{1,0:T(1,128)S(1)} %broadcast_in_dim_reshape.7.bias_ref, bf16[128,128]{1,0:T(8,128)(2,1)S(1)} %bitcast.20), custom_call_target="tpu_custom_call" | custom-call | tf_op jit(solution)/shard_map/updates/pallas_call | solution.py:284
  119.1 34.6 %all_to_all.16.u_ref = bf16[128,64,128]{2,1,0:T(8,128)(2,1)S(1)} all-to-all(bf16[128,64,128]{2,1,0:T(8,128)(2,1)S(1)} %bitcast.19), channel_id=1, replica_groups=mesh['dap'=32,'rep'=4] {'dap','rep'}, dimensions={0} | all-to-all | bytes 4194304 | tf_op jit(solution)/shard_map/all_to_all | solution.py:328
  153.7 1.8 %place.1 = bf16[32,32,1024]{2,1,0:T(8,128)(2,1)} custom-call(bf16[128,64,128]{2,1,0:T(8,128)(2,1)S(1)} %all_to_all.16.u_ref), custom_call_target="tpu_custom_call" | custom-call | tf_op jit(solution)/shard_map/place/pallas_call | solution.py:316
  (8 shorter events, 0.0 us)
Async XLA Ops:
  0.0 15.4 %collective-permute-start = (bf16[32,128]{1,0:T(8,128)(2,1)}, bf16[32,128]{1,0:T(8,128)(2,1)S(1)}, u32[]{:S(2)}, u32[]{:S(2)}) collective-permute-start(bf16[32,128]{1,0:T(8,128)(2,1)} %bitcast.21), channel_id=1, source_target_pairs={{0,1},{1,2},{2,3},{3,0},{4,5},{5,6},{6,7},{7,4},{8,9},{9,10},{10,1... | collective-permute-start | bytes 24584 | tf_op jit(solution)/shard_map/ppermute | solution.py:334
  4.1 11.3 %collective-permute-start.1 = (bf16[32,128]{1,0:T(8,128)(2,1)}, bf16[32,128]{1,0:T(8,128)(2,1)S(1)}, u32[]{:S(2)}, u32[]{:S(2)}) collective-permute-start(bf16[32,128]{1,0:T(8,128)(2,1)} %bitcast.22), channel_id=1, source_target_pairs={{0,2},{1,3},{2,0},{3,1},{4,6},{5,7},{6,4},{7,5},{8,10},{9,11},{10,... | collective-permute-start | bytes 24584 | tf_op jit(solution)/shard_map/ppermute | solution.py:334
  4.3 11.1 %collective-permute-start.2 = (bf16[32,128]{1,0:T(8,128)(2,1)}, bf16[32,128]{1,0:T(8,128)(2,1)S(1)}, u32[]{:S(2)}, u32[]{:S(2)}) collective-permute-start(bf16[32,128]{1,0:T(8,128)(2,1)} %bitcast.23), channel_id=1, source_target_pairs={{0,3},{1,0},{2,1},{3,2},{4,7},{5,4},{6,5},{7,6},{8,11},{9,8},{10,9... | collective-permute-start | bytes 24584 | tf_op jit(solution)/shard_map/ppermute | solution.py:334
  74.8 9.5 %copy-start.2 = (f32[128]{0:T(128)S(1)}, f32[128]{0:T(128)}, u32[]{:S(2)}) copy-start(f32[128]{0:T(128)} %param.23) | copy-start | bytes 1540
  74.8 9.8 %copy-start.3 = (f32[128]{0:T(128)S(1)}, f32[128]{0:T(128)}, u32[]{:S(2)}) copy-start(f32[128]{0:T(128)} %param.24) | copy-start | bytes 1540
  74.9 10.1 %copy-start.1 = (bf16[128,128]{1,0:T(8,128)(2,1)S(1)}, bf16[128,128]{1,0:T(8,128)(2,1)}, u32[]{:S(2)}) copy-start(bf16[128,128]{1,0:T(8,128)(2,1)} %param.25) | copy-start | bytes 98308
  74.9 10.2 %copy-start = (bf16[128,32]{0,1:T(8,128)(2,1)S(1)}, bf16[128,32]{0,1:T(8,128)(2,1)}, u32[]{:S(2)}) copy-start(bf16[128,32]{0,1:T(8,128)(2,1)} %param.22) | copy-start | bytes 24580
  74.9 39.5 %all-to-all-start.1 = ((bf16[128,8,1024]{2,1,0:T(8,128)(2,1)}), bf16[128,8,1024]{2,1,0:T(8,128)(2,1)S(1)}, u32[]{:S(2)}, u32[]{:S(2)}) async-start(bf16[128,8,1024]{2,1,0:T(8,128)(2,1)} %products.1), calls=%async_computation.1 | async-start | bytes 4194304 | tf_op jit(solution)/shard_map/all_to_all | solution.py:328

commit v5 on v4

--- a/solution.py
+++ b/solution.py
@@ -152,7 +152,8 @@
         y = jnp.dot(weights, normed_columns(x_ref[i], gain, bias), preferred_element_type=f32)
         result = 0.5 * jnp.tanh(0.5 * y) + 0.5
         for shift in range(len(parts)):
-            owner = lax.rem(where[1] - shift + len(parts), len(parts))
+            high, low = lax.div(where[1], 2), lax.rem(where[1], 2)
+            owner = 2 * (1 - high if shift & 2 else high) + (1 - low if shift & 1 else low)
             for part in range(tile // lane):
                 held[part, pl.ds(owner * (each * step) + i, each, stride=step), :] = result[
                     shift * each : (shift + 1) * each, part * lane : (part + 1) * lane
@@ -298,43 +299,41 @@
     )(near(product), stay(gating), gain, bias, weights)
 
 
-def place_kernel(u_ref, out_ref):
+def place_kernel(u_ref, out_hbm, out_ref, sems, *, share):
     blocks, rows, lanes = u_ref.shape
-    groups = out_ref.shape[0] // pack
-    share = rows // groups
-    for g in range(groups):
+    copies = []
+    for g in range(rows // share):
         flat = u_ref[:, g * share : (g + 1) * share, :].astype(f32).reshape(blocks * share, lanes)
-        out_ref[pack * g : pack * (g + 1)] = flat.T.astype(bf16).reshape(
-            pack, lanes // pack, blocks * share
-        )
-
-
-def place(received, share, each):
+        at = pl.ds(g * pack, pack)
+        out_ref[at] = flat.T.astype(bf16).reshape(pack, lanes // pack, blocks * share)
+        copies.append(pltpu.make_async_copy(out_ref.at[at], out_hbm.at[at], sems.at[g]))
+        copies[-1].start()
+    for copy in copies:
+        copy.wait()
+
+
+def place(received, share):
     blocks, rows, lanes = received.shape
-    groups = rows // share
-    shape = (lanes // pack, blocks * share)
+    shape = (rows // share * pack, lanes // pack, blocks * share)
     return pl.pallas_call(
-        place_kernel,
-        grid=(groups // each,),
-        in_specs=[pl.BlockSpec((blocks, share * each, lanes), lambda g: (0, g, 0))],
-        out_specs=pl.BlockSpec((pack * each, *shape), lambda g: (g, 0, 0)),
-        out_shape=jax.ShapeDtypeStruct((groups * pack, *shape), bf16),
+        functools.partial(place_kernel, share=share),
+        in_specs=[whole],
+        out_specs=pl.BlockSpec(memory_space=pltpu.HBM),
+        out_shape=pltpu.HBM(shape, bf16),
+        scratch_shapes=[pltpu.VMEM(shape, bf16), pltpu.SemaphoreType.DMA((rows // share,))],
         compiler_params=params(20),
         name="place",
-    )(received)
+    )(near(received))
 
 
 def exchange(blocks, axes):
     return lax.all_to_all(blocks, axes, split_axis=0, concat_axis=0, tiled=True)
 
 
-def from_before(own, axis):
-    count = lax.axis_size(axis)
-    parts = [
-        lax.ppermute(own, axis, [(k, (k + shift) % count) for k in range(count)])
-        for shift in range(count - 1, 0, -1)
+def from_peers(own):
+    return [own] + [
+        lax.ppermute(own, "rep", [(k, k ^ distance) for k in range(4)]) for distance in (1, 2, 3)
     ]
-    return [own] + parts[::-1]
 
 
 def on_device(
@@ -357,7 +356,7 @@
     share = rows // parts
     where = jnp.stack([lax.axis_index("dap"), lax.axis_index("rep")]).astype(jnp.int32)
     gain_in, bias_in = input_gain[None], input_bias[None]
-    all_gates = from_before(gate_weight.T, "rep")
+    all_gates = from_peers(gate_weight.T)
     both = project(
         where,
         residue_mask,
@@ -389,7 +388,7 @@
         256,
     )
     update = exchange(update.reshape(total // share, -1, lane), everyone)
-    return jnp.swapaxes(place(update, share, 4), 1, 2)
+    return jnp.swapaxes(place(update, share), 1, 2)
 
 
 def solution(mesh):

time: 156 us -> 156 us (level)
  blocking collectives: 90.9 us -> 93.1 us
  starting transfers between devices: 14.1 us -> 12.2 us
    all_to_all x2, blocking collectives: 90.9 us -> 93.1 us  [exchange(): return lax.all_to_all(blocks, axes, split_axis=0, concat_axis=0, tiled=True)]
    all_to_all x1, starting transfers between devices: 9.49 us -> 7.69 us  [exchange(): return lax.all_to_all(blocks, axes, split_axis=0, concat_axis=0, tiled=True)]
where the time goes in v5:
time: 156 us
  blocking collectives  93.1 us (60%)
  Pallas kernels  26.5 us (17%)
  waiting for transfers between devices  22.9 us (15%)
  starting transfers between devices  12.2 us (8%)
    all_to_all x2, blocking collectives, exchange(): return lax.all_to_all(blocks, axes, split_axis=0, concat_axis=0, tiled=True)  93.1 us
    all_to_all x1, waiting for transfers between devices, exchange(): return lax.all_to_all(blocks, axes, split_axis=0, concat_axis=0, tiled=True)  22.9 us
    pallas_call x1, Pallas kernels, project(): pl.pallas_call(project_kernel, grid_spec=pltpu.PrefetchScalarGridSpec(num...  10.7 us
    all_to_all x1, starting transfers between devices, exchange(): return lax.all_to_all(blocks, axes, split_axis=0, concat_axis=0, tiled=True)  7.69 us
    pallas_call x1, Pallas kernels, gates(): pl.pallas_call(gate_kernel, grid_spec=pltpu.PrefetchScalarGridSpec(num_sc...  6.39 us
    pallas_call x1, Pallas kernels, updates(): pl.pallas_call(functools.partial(update_kernel, tile=tile), in_specs=[who...  4.69 us
    ppermute x3, starting transfers between devices, from_peers(): lax.ppermute(own, 'rep', [(k, k ^ distance) for k in range(4)])  4.56 us
    pallas_call x1, Pallas kernels, products(): pl.pallas_call(functools.partial(product_kernel, counts=counts), in_specs...  3.18 us
  transfers between devices with their start and end apart: 4, of which 1 were waited for; matrix products, arithmetic and copies ran while one was open for 0% of the time, Pallas kernels for 11%

profile of v5, /device:TPU:1, one launch (start us, length us, event | category | flops | bytes accessed | tf_op | source)
XLA Modules:
  0.0 155.7 jit_solution(16075006709700238990)
XLA Ops:
  0.0 1.4 collective-permute-start
  1.4 2.8 %collective-permute-start.1 = (bf16[32,128]{1,0:T(8,128)(2,1)}, bf16[32,128]{1,0:T(8,128)(2,1)S(1)}, u32[]{:S(2)}, u32[]{:S(2)}) collective-permute-start(bf16[32,128]{1,0:T(8,128)(2,1)} %bitcast.22), channel_id=1, source_target_pairs={{0,2},{1,3},{2,0},{3,1},{4,6},{5,7},{6,4},{7,5},{8,10},{9,11},{10,... | collective-permute-start | bytes 24584 | tf_op jit(solution)/shard_map/ppermute | solution.py:335
  4.2 0.3 collective-permute-start.2
  4.6 0.1 pad_add_fusion.where
  4.6 10.7 %project.1 = bf16[32,2,32,1024]{3,2,1,0:T(8,128)(2,1)S(1)} custom-call(s32[2]{0:T(128)S(1)} %pad_add_fusion.where, s32[1024]{0:T(1024)} %residues.1, bf16[32,1024,128]{2,1,0:T(8,128)(2,1)} %x_ref.3, bf16[32,128]{1,0:T(8,128)(2,1)} %bitcast.30, bf16[32,128]{1,0:T(8,128)(2,1)} %bitcast.31, bf16[32,128]{1,0:T(8,128)(2,1)} %bitcast.32, ...), custom_call_target="tpu_custom_call" | custom-call | tf_op jit(solution)/shard_map/project/pallas_call | solution.py:112
  15.4 58.5 %all_to_all.15.both_ref = bf16[32,2,32,1024]{3,2,1,0:T(8,128)(2,1)S(1)} all-to-all(bf16[32,2,32,1024]{3,2,1,0:T(8,128)(2,1)S(1)} %project.1), channel_id=1, replica_groups=mesh['dap'=32,'rep'=4] {'dap'}, dimensions={0} | all-to-all | bytes 8388608 | tf_op jit(solution)/shard_map/all_to_all | solution.py:330
  73.9 3.2 %products.1 = bf16[128,8,1024]{2,1,0:T(8,128)(2,1)} custom-call(bf16[32,2,32,1024]{3,2,1,0:T(8,128)(2,1)S(1)} %all_to_all.15.both_ref), custom_call_target="tpu_custom_call" | custom-call | tf_op jit(solution)/shard_map/products/pallas_call | solution.py:215
  77.1 0.0 copy-start.2
  77.1 0.0 copy-start.3
  77.1 0.0 copy-start.1
  77.1 0.0 copy-start
  77.1 7.7 %all-to-all-start.1 = ((bf16[128,8,1024]{2,1,0:T(8,128)(2,1)}), bf16[128,8,1024]{2,1,0:T(8,128)(2,1)S(1)}, u32[]{:S(2)}, u32[]{:S(2)}) async-start(bf16[128,8,1024]{2,1,0:T(8,128)(2,1)} %products.1), calls=%async_computation.1 | async-start | bytes 4194304 | tf_op jit(solution)/shard_map/all_to_all | solution.py:330
  84.8 0.1 reshape.15
  84.9 0.1 copy.17
  85.0 0.1 broadcast_in_dim_reshape.6.gain_ref
  85.1 0.1 reshape.16
  85.2 0.1 copy.18
  85.3 0.1 broadcast_in_dim_reshape.7.bias_ref
  85.5 0.1 copy.20
  85.6 6.4 %gates.1.gate_hbm = bf16[4,128,8,256]{3,2,1,0:T(8,128)(2,1)} custom-call(s32[2]{0:T(128)S(1)} %pad_add_fusion.where, bf16[32,1024,128]{2,1,0:T(8,128)(2,1)} %x_ref.3, bf16[32,128]{1,0:T(8,128)(2,1)S(1)} %bitcast.24, bf16[32,128]{1,0:T(8,128)(2,1)S(1)} %collective-permute-done.w1, bf16[32,128]{1,0:T(8,128)(2,1)S(1)} %collective-permute-done.1.w2, ...), custom_call_target="tpu_custom_call" | custom-call | flops 268435456 | bytes 4194304 | tf_op jit(solution)/shard_map/gates/pallas_call | solution.py:172
  92.0 22.9 %all-to-all-done.1.p_ref = bf16[128,8,1024]{2,1,0:T(8,128)(2,1)S(1)} async-done(((bf16[128,8,1024]{2,1,0:T(8,128)(2,1)}), bf16[128,8,1024]{2,1,0:T(8,128)(2,1)S(1)}, u32[]{:S(2)}, u32[]{:S(2)}) %all-to-all-start.1) | async-done | bytes 2097184 | tf_op jit(solution)/shard_map/all_to_all | solution.py:330
  114.9 4.7 %updates.1 = bf16[32,256,128]{2,1,0:T(8,128)(2,1)S(1)} custom-call(bf16[128,8,1024]{2,1,0:T(8,128)(2,1)S(1)} %all-to-all-done.1.p_ref, bf16[4,128,8,256]{3,2,1,0:T(8,128)(2,1)} %gates.1.gate_hbm, f32[1,128]{1,0:T(1,128)S(1)} %broadcast_in_dim_reshape.6.gain_ref, f32[1,128]{1,0:T(1,128)S(1)} %broadcast_in_dim_reshape.7.bias_ref, bf16[128,128]{1,0:T(8,128)(2,1)S(1)} %bitcast.20), custom_call_target="tpu_custom_call" | custom-call | tf_op jit(solution)/shard_map/updates/pallas_call | solution.py:285
  119.6 34.6 %all_to_all.16.u_ref = bf16[128,64,128]{2,1,0:T(8,128)(2,1)S(1)} all-to-all(bf16[128,64,128]{2,1,0:T(8,128)(2,1)S(1)} %bitcast.19), channel_id=1, replica_groups=mesh['dap'=32,'rep'=4] {'dap','rep'}, dimensions={0} | all-to-all | bytes 4194304 | tf_op jit(solution)/shard_map/all_to_all | solution.py:330
  154.2 1.5 place.1
  (8 shorter events, 0.0 us)
Async XLA Ops:
  0.0 15.4 %collective-permute-start = (bf16[32,128]{1,0:T(8,128)(2,1)}, bf16[32,128]{1,0:T(8,128)(2,1)S(1)}, u32[]{:S(2)}, u32[]{:S(2)}) collective-permute-start(bf16[32,128]{1,0:T(8,128)(2,1)} %bitcast.21), channel_id=1, source_target_pairs={{0,1},{1,0},{2,3},{3,2},{4,5},{5,4},{6,7},{7,6},{8,9},{9,8},{10,11... | collective-permute-start | bytes 24584 | tf_op jit(solution)/shard_map/ppermute | solution.py:335
  1.4 14.0 %collective-permute-start.1 = (bf16[32,128]{1,0:T(8,128)(2,1)}, bf16[32,128]{1,0:T(8,128)(2,1)S(1)}, u32[]{:S(2)}, u32[]{:S(2)}) collective-permute-start(bf16[32,128]{1,0:T(8,128)(2,1)} %bitcast.22), channel_id=1, source_target_pairs={{0,2},{1,3},{2,0},{3,1},{4,6},{5,7},{6,4},{7,5},{8,10},{9,11},{10,... | collective-permute-start | bytes 24584 | tf_op jit(solution)/shard_map/ppermute | solution.py:335
  4.2 11.1 %collective-permute-start.2 = (bf16[32,128]{1,0:T(8,128)(2,1)}, bf16[32,128]{1,0:T(8,128)(2,1)S(1)}, u32[]{:S(2)}, u32[]{:S(2)}) collective-permute-start(bf16[32,128]{1,0:T(8,128)(2,1)} %bitcast.23), channel_id=1, source_target_pairs={{0,3},{1,2},{2,1},{3,0},{4,7},{5,6},{6,5},{7,4},{8,11},{9,10},{10,... | collective-permute-start | bytes 24584 | tf_op jit(solution)/shard_map/ppermute | solution.py:335
  77.1 7.7 %copy-start.2 = (f32[128]{0:T(128)S(1)}, f32[128]{0:T(128)}, u32[]{:S(2)}) copy-start(f32[128]{0:T(128)} %param.23) | copy-start | bytes 1540
  77.1 8.0 %copy-start.3 = (f32[128]{0:T(128)S(1)}, f32[128]{0:T(128)}, u32[]{:S(2)}) copy-start(f32[128]{0:T(128)} %param.24) | copy-start | bytes 1540
  77.1 8.3 %copy-start.1 = (bf16[128,128]{1,0:T(8,128)(2,1)S(1)}, bf16[128,128]{1,0:T(8,128)(2,1)}, u32[]{:S(2)}) copy-start(bf16[128,128]{1,0:T(8,128)(2,1)} %param.25) | copy-start | bytes 98308
  77.1 8.4 %copy-start = (bf16[128,32]{0,1:T(8,128)(2,1)S(1)}, bf16[128,32]{0,1:T(8,128)(2,1)}, u32[]{:S(2)}) copy-start(bf16[128,32]{0,1:T(8,128)(2,1)} %param.22) | copy-start | bytes 24580
  77.1 37.7 %all-to-all-start.1 = ((bf16[128,8,1024]{2,1,0:T(8,128)(2,1)}), bf16[128,8,1024]{2,1,0:T(8,128)(2,1)S(1)}, u32[]{:S(2)}, u32[]{:S(2)}) async-start(bf16[128,8,1024]{2,1,0:T(8,128)(2,1)} %products.1), calls=%async_computation.1 | async-start | bytes 4194304 | tf_op jit(solution)/shard_map/all_to_all | solution.py:330

commit v6 on v5

--- a/solution.py
+++ b/solution.py
@@ -378,7 +378,7 @@
             values.shape
         )
 
-    product = exchange(products(both, share, (24, 8)), everyone)
+    product = exchange(products(both, share, (28, 4)), everyone)
     update = updates(
         product,
         gating,

time: 156 us -> 156 us (level)
  no operation moved by 1% of the time
where the time goes in v6:
time: 156 us
  blocking collectives  93.1 us (60%)
  Pallas kernels  26.8 us (17%)
  waiting for transfers between devices  22.9 us (15%)
  starting transfers between devices  12.2 us (8%)
    all_to_all x2, blocking collectives, exchange(): return lax.all_to_all(blocks, axes, split_axis=0, concat_axis=0, tiled=True)  93.1 us
    all_to_all x1, waiting for transfers between devices, exchange(): return lax.all_to_all(blocks, axes, split_axis=0, concat_axis=0, tiled=True)  22.9 us
    pallas_call x1, Pallas kernels, project(): pl.pallas_call(project_kernel, grid_spec=pltpu.PrefetchScalarGridSpec(num...  10.7 us
    all_to_all x1, starting transfers between devices, exchange(): return lax.all_to_all(blocks, axes, split_axis=0, concat_axis=0, tiled=True)  7.69 us
    pallas_call x1, Pallas kernels, gates(): pl.pallas_call(gate_kernel, grid_spec=pltpu.PrefetchScalarGridSpec(num_sc...  6.39 us
    pallas_call x1, Pallas kernels, updates(): pl.pallas_call(functools.partial(update_kernel, tile=tile), in_specs=[who...  4.69 us
    ppermute x3, starting transfers between devices, from_peers(): lax.ppermute(own, 'rep', [(k, k ^ distance) for k in range(4)])  4.56 us
    pallas_call x1, Pallas kernels, products(): pl.pallas_call(functools.partial(product_kernel, counts=counts), in_specs...  3.44 us
  transfers between devices with their start and end apart: 4, of which 1 were waited for; matrix products, arithmetic and copies ran while one was open for 0% of the time, Pallas kernels for 11%

profile of v6, /device:TPU:1, one launch (start us, length us, event | category | flops | bytes accessed | tf_op | source)
XLA Modules:
  0.0 156.0 jit_solution(3178965075489149912)
XLA Ops:
  0.0 1.4 collective-permute-start
  1.4 2.8 %collective-permute-start.1 = (bf16[32,128]{1,0:T(8,128)(2,1)}, bf16[32,128]{1,0:T(8,128)(2,1)S(1)}, u32[]{:S(2)}, u32[]{:S(2)}) collective-permute-start(bf16[32,128]{1,0:T(8,128)(2,1)} %bitcast.22), channel_id=1, source_target_pairs={{0,2},{1,3},{2,0},{3,1},{4,6},{5,7},{6,4},{7,5},{8,10},{9,11},{10,... | collective-permute-start | bytes 24584 | tf_op jit(solution)/shard_map/ppermute | solution.py:335
  4.2 0.3 collective-permute-start.2
  4.6 0.1 pad_add_fusion.where
  4.6 10.7 %project.1 = bf16[32,2,32,1024]{3,2,1,0:T(8,128)(2,1)S(1)} custom-call(s32[2]{0:T(128)S(1)} %pad_add_fusion.where, s32[1024]{0:T(1024)} %residues.1, bf16[32,1024,128]{2,1,0:T(8,128)(2,1)} %x_ref.3, bf16[32,128]{1,0:T(8,128)(2,1)} %bitcast.30, bf16[32,128]{1,0:T(8,128)(2,1)} %bitcast.31, bf16[32,128]{1,0:T(8,128)(2,1)} %bitcast.32, ...), custom_call_target="tpu_custom_call" | custom-call | tf_op jit(solution)/shard_map/project/pallas_call | solution.py:112
  15.4 58.5 %all_to_all.15.both_ref = bf16[32,2,32,1024]{3,2,1,0:T(8,128)(2,1)S(1)} all-to-all(bf16[32,2,32,1024]{3,2,1,0:T(8,128)(2,1)S(1)} %project.1), channel_id=1, replica_groups=mesh['dap'=32,'rep'=4] {'dap'}, dimensions={0} | all-to-all | bytes 8388608 | tf_op jit(solution)/shard_map/all_to_all | solution.py:330
  73.9 3.4 %products.1 = bf16[128,8,1024]{2,1,0:T(8,128)(2,1)} custom-call(bf16[32,2,32,1024]{3,2,1,0:T(8,128)(2,1)S(1)} %all_to_all.15.both_ref), custom_call_target="tpu_custom_call" | custom-call | tf_op jit(solution)/shard_map/products/pallas_call | solution.py:215
  77.4 0.0 copy-start.2
  77.4 0.0 copy-start.3
  77.4 0.0 copy-start.1
  77.4 0.0 copy-start
  77.4 7.7 %all-to-all-start.1 = ((bf16[128,8,1024]{2,1,0:T(8,128)(2,1)}), bf16[128,8,1024]{2,1,0:T(8,128)(2,1)S(1)}, u32[]{:S(2)}, u32[]{:S(2)}) async-start(bf16[128,8,1024]{2,1,0:T(8,128)(2,1)} %products.1), calls=%async_computation.1 | async-start | bytes 4194304 | tf_op jit(solution)/shard_map/all_to_all | solution.py:330
  85.1 0.1 reshape.15
  85.2 0.1 copy.17
  85.3 0.1 broadcast_in_dim_reshape.6.gain_ref
  85.4 0.1 reshape.16
  85.5 0.1 copy.18
  85.6 0.1 broadcast_in_dim_reshape.7.bias_ref
  85.7 0.1 copy.20
  85.8 6.4 %gates.1.gate_hbm = bf16[4,128,8,256]{3,2,1,0:T(8,128)(2,1)} custom-call(s32[2]{0:T(128)S(1)} %pad_add_fusion.where, bf16[32,1024,128]{2,1,0:T(8,128)(2,1)} %x_ref.3, bf16[32,128]{1,0:T(8,128)(2,1)S(1)} %bitcast.24, bf16[32,128]{1,0:T(8,128)(2,1)S(1)} %collective-permute-done.w1, bf16[32,128]{1,0:T(8,128)(2,1)S(1)} %collective-permute-done.1.w2, ...), custom_call_target="tpu_custom_call" | custom-call | flops 268435456 | bytes 4194304 | tf_op jit(solution)/shard_map/gates/pallas_call | solution.py:172
  92.2 22.9 %all-to-all-done.1.p_ref = bf16[128,8,1024]{2,1,0:T(8,128)(2,1)S(1)} async-done(((bf16[128,8,1024]{2,1,0:T(8,128)(2,1)}), bf16[128,8,1024]{2,1,0:T(8,128)(2,1)S(1)}, u32[]{:S(2)}, u32[]{:S(2)}) %all-to-all-start.1) | async-done | bytes 2097184 | tf_op jit(solution)/shard_map/all_to_all | solution.py:330
  115.1 4.7 %updates.1 = bf16[32,256,128]{2,1,0:T(8,128)(2,1)S(1)} custom-call(bf16[128,8,1024]{2,1,0:T(8,128)(2,1)S(1)} %all-to-all-done.1.p_ref, bf16[4,128,8,256]{3,2,1,0:T(8,128)(2,1)} %gates.1.gate_hbm, f32[1,128]{1,0:T(1,128)S(1)} %broadcast_in_dim_reshape.6.gain_ref, f32[1,128]{1,0:T(1,128)S(1)} %broadcast_in_dim_reshape.7.bias_ref, bf16[128,128]{1,0:T(8,128)(2,1)S(1)} %bitcast.20), custom_call_target="tpu_custom_call" | custom-call | tf_op jit(solution)/shard_map/updates/pallas_call | solution.py:285
  119.8 34.6 %all_to_all.16.u_ref = bf16[128,64,128]{2,1,0:T(8,128)(2,1)S(1)} all-to-all(bf16[128,64,128]{2,1,0:T(8,128)(2,1)S(1)} %bitcast.19), channel_id=1, replica_groups=mesh['dap'=32,'rep'=4] {'dap','rep'}, dimensions={0} | all-to-all | bytes 4194304 | tf_op jit(solution)/shard_map/all_to_all | solution.py:330
  154.5 1.5 place.1
  (8 shorter events, 0.0 us)
Async XLA Ops:
  0.0 15.4 %collective-permute-start = (bf16[32,128]{1,0:T(8,128)(2,1)}, bf16[32,128]{1,0:T(8,128)(2,1)S(1)}, u32[]{:S(2)}, u32[]{:S(2)}) collective-permute-start(bf16[32,128]{1,0:T(8,128)(2,1)} %bitcast.21), channel_id=1, source_target_pairs={{0,1},{1,0},{2,3},{3,2},{4,5},{5,4},{6,7},{7,6},{8,9},{9,8},{10,11... | collective-permute-start | bytes 24584 | tf_op jit(solution)/shard_map/ppermute | solution.py:335
  1.4 14.0 %collective-permute-start.1 = (bf16[32,128]{1,0:T(8,128)(2,1)}, bf16[32,128]{1,0:T(8,128)(2,1)S(1)}, u32[]{:S(2)}, u32[]{:S(2)}) collective-permute-start(bf16[32,128]{1,0:T(8,128)(2,1)} %bitcast.22), channel_id=1, source_target_pairs={{0,2},{1,3},{2,0},{3,1},{4,6},{5,7},{6,4},{7,5},{8,10},{9,11},{10,... | collective-permute-start | bytes 24584 | tf_op jit(solution)/shard_map/ppermute | solution.py:335
  4.2 11.1 %collective-permute-start.2 = (bf16[32,128]{1,0:T(8,128)(2,1)}, bf16[32,128]{1,0:T(8,128)(2,1)S(1)}, u32[]{:S(2)}, u32[]{:S(2)}) collective-permute-start(bf16[32,128]{1,0:T(8,128)(2,1)} %bitcast.23), channel_id=1, source_target_pairs={{0,3},{1,2},{2,1},{3,0},{4,7},{5,6},{6,5},{7,4},{8,11},{9,10},{10,... | collective-permute-start | bytes 24584 | tf_op jit(solution)/shard_map/ppermute | solution.py:335
  77.4 7.7 %copy-start.2 = (f32[128]{0:T(128)S(1)}, f32[128]{0:T(128)}, u32[]{:S(2)}) copy-start(f32[128]{0:T(128)} %param.23) | copy-start | bytes 1540
  77.4 8.0 %copy-start.3 = (f32[128]{0:T(128)S(1)}, f32[128]{0:T(128)}, u32[]{:S(2)}) copy-start(f32[128]{0:T(128)} %param.24) | copy-start | bytes 1540
  77.4 8.3 %copy-start.1 = (bf16[128,128]{1,0:T(8,128)(2,1)S(1)}, bf16[128,128]{1,0:T(8,128)(2,1)}, u32[]{:S(2)}) copy-start(bf16[128,128]{1,0:T(8,128)(2,1)} %param.25) | copy-start | bytes 98308
  77.4 8.4 %copy-start = (bf16[128,32]{0,1:T(8,128)(2,1)S(1)}, bf16[128,32]{0,1:T(8,128)(2,1)}, u32[]{:S(2)}) copy-start(bf16[128,32]{0,1:T(8,128)(2,1)} %param.22) | copy-start | bytes 24580
  77.4 37.7 %all-to-all-start.1 = ((bf16[128,8,1024]{2,1,0:T(8,128)(2,1)}), bf16[128,8,1024]{2,1,0:T(8,128)(2,1)S(1)}, u32[]{:S(2)}, u32[]{:S(2)}) async-start(bf16[128,8,1024]{2,1,0:T(8,128)(2,1)} %products.1), calls=%async_computation.1 | async-start | bytes 4194304 | tf_op jit(solution)/shard_map/all_to_all | solution.py:330
